TPU v7x, 256 devices: a whole 4x4x8 slice. The times are simulated.
256 devices in a mesh: frames: 16 (over z, core), heads: 4 (over x), dp: 4 (over y).
Axes of the slice: x: 4, y: 4, z: 8, core: 2. Of those that a mesh axis runs over, the one named last changes fastest.
Arguments:
- queries: bfloat16 [10240, 4096], P(('dp', 'frames'), 'heads'), parts along dimension 0, may hold values from -10 to 10
- key_vectors: bfloat16 [10240, 4096], P(('dp', 'frames'), 'heads'), parts along dimension 0, may hold values from -4 to 4
- values: bfloat16 [10240, 4096], P(('dp', 'frames'), 'heads'), parts along dimension 0, may hold values from -5 to 5
- grad_output: bfloat16 [10240, 4096], P(('dp', 'frames'), 'heads'), parts along dimension 0, may hold values from -5 to 5
- segment_index: int32 [10240], P(('dp', 'frames')), parts along dimension 0, may hold values from 0 to 63, as said below
Outputs:
- attended: bfloat16 [10240, 4096], P(('dp', 'frames'), 'heads'), parts along dimension 0
- grad_queries: bfloat16 [10240, 4096], P(('dp', 'frames'), 'heads'), parts along dimension 0
- grad_keys: bfloat16 [10240, 4096], P(('dp', 'frames'), 'heads'), parts along dimension 0
- grad_values: bfloat16 [10240, 4096], P(('dp', 'frames'), 'heads'), parts along dimension 0
There are 4 independent parts, one for each index of `dp`. A program takes and returns all parts, laid end to end along the dimension named above; each array names one. Nothing has to cross between parts.
Inputs may be any that keep to these rules, and one draw needn't show every extreme that they name: `segment_index`: rows are stored in paired order: the first 80 rows of frames index g are the natural positions g * 80 onward, its last 80 rows the positions (31 - g) * 80 onward. Along natural positions the segment never falls, starts at 0 (the reference-image prefix), and each of the 64 segments holds at least one position.
All inputs are finite; a program needn't handle non-finite values.
Results may differ from a plain program's by a relative error of at most 0.014.
Values may be sent and summed in bfloat16 or wider, within the bound.
A program may use at most 128 MiB of HBM per device.

v0:
```python
import math

import jax
import jax.numpy as jnp
from jax import lax
from jax.sharding import PartitionSpec as P

HEAD_DIM = 128


def head_split(array):
    return array.reshape(array.shape[0], array.shape[1] // HEAD_DIM, HEAD_DIM)


def natural_order(array, shard_count, row_count):
    half_rows = row_count // 2
    parts = array.reshape((shard_count, 2, half_rows) + array.shape[1:])
    joined = jnp.concatenate([parts[:, 0], jnp.flip(parts[:, 1], axis=0)], axis=0)
    return joined.reshape((shard_count * row_count,) + array.shape[1:])


def paired_order(array, shard_count, row_count):
    half_rows = row_count // 2
    parts = array.reshape((2 * shard_count, half_rows) + array.shape[1:])
    lower = parts[:shard_count]
    upper = jnp.flip(parts[shard_count:], axis=0)
    return jnp.stack([lower, upper], axis=1).reshape((shard_count * row_count,) + array.shape[1:])


def score_block(query_heads, key_heads):
    product = jnp.einsum("qhd,khd->qhk", query_heads, key_heads, preferred_element_type=jnp.float32)
    return product * (1.0 / math.sqrt(HEAD_DIM))


def visible(query_segment, key_segment):
    return key_segment[None, None, :] <= query_segment[:, None, None]


def weights_of(query_heads, query_segment, log_total, key_heads, key_segment):
    scores = score_block(query_heads, key_heads)
    return jnp.where(
        visible(query_segment, key_segment), jnp.exp(scores - log_total[:, :, None]), 0.0
    )


def grad_parts(
    query_heads,
    grad_heads,
    query_segment,
    log_total,
    row_delta,
    key_heads,
    value_heads,
    key_segment,
):
    soft_weights = weights_of(query_heads, query_segment, log_total, key_heads, key_segment)
    grad_weights = jnp.einsum(
        "qhd,khd->qhk", grad_heads, value_heads, preferred_element_type=jnp.float32
    )
    grad_scores = (soft_weights * (grad_weights - row_delta[:, :, None])).astype(jnp.bfloat16)
    return (soft_weights.astype(jnp.bfloat16), grad_scores)


def shards(queries, key_vectors, values, grad_output, segment_index):
    row_count, full_width = queries.shape
    head_count = full_width // HEAD_DIM
    shard_count = lax.axis_size("frames")
    scale_factor = 1.0 / math.sqrt(HEAD_DIM)
    query_heads = head_split(queries)
    grad_heads = head_split(grad_output)
    own_segment = segment_index.astype(jnp.float32)
    own_top = jnp.max(own_segment)
    segment_tags = segment_index.astype(jnp.bfloat16)
    key_whole, value_whole, key_tags = (
        lax.all_gather(key_vectors, "frames", axis=0, tiled=True),
        lax.all_gather(values, "frames", axis=0, tiled=True),
        lax.all_gather(segment_tags, "frames", axis=0, tiled=True),
    )
    key_total = key_whole.shape[0]
    key_span = min(key_total, 4 * row_count)
    span_count = key_total // key_span
    key_heads_all = head_split(natural_order(key_whole, shard_count, row_count))
    value_heads_all = head_split(natural_order(value_whole, shard_count, row_count))
    key_segment_all = natural_order(key_tags, shard_count, row_count).astype(jnp.float32)

    def key_slice(block_index):
        first_row = block_index * key_span
        return (
            lax.dynamic_slice_in_dim(key_heads_all, first_row, key_span, 0),
            lax.dynamic_slice_in_dim(value_heads_all, first_row, key_span, 0),
            lax.dynamic_slice_in_dim(key_segment_all, first_row, key_span, 0),
        )

    def span_seen(key_segment):
        return jnp.min(key_segment) <= own_top

    def stats_step(block_index, loop_state):
        key_heads, value_heads, key_segment = key_slice(block_index)

        def stats_work(state):
            running_max, running_sum = state
            seen_mask = visible(own_segment, key_segment)
            scores = jnp.where(seen_mask, score_block(query_heads, key_heads), -1e30)
            new_max = jnp.maximum(running_max, jnp.max(scores, axis=2))
            added = jnp.sum(
                jnp.where(seen_mask, jnp.exp(scores - new_max[:, :, None]), 0.0), axis=2
            )
            return (new_max, running_sum * jnp.exp(running_max - new_max) + added)

        return lax.cond(span_seen(key_segment), stats_work, lambda state: state, loop_state)

    start_max = jnp.full((row_count, head_count), -1e30, jnp.float32)
    start_sum = jnp.zeros((row_count, head_count), jnp.float32)
    running_max, running_sum = lax.fori_loop(0, span_count, stats_step, (start_max, start_sum))
    log_total = running_max + jnp.log(running_sum)

    def output_step(block_index, total_acc):
        key_heads, value_heads, key_segment = key_slice(block_index)

        def output_work(acc):
            weights_low = weights_of(
                query_heads, own_segment, log_total, key_heads, key_segment
            ).astype(jnp.bfloat16)
            return acc + jnp.einsum(
                "qhk,khd->qhd", weights_low, value_heads, preferred_element_type=jnp.float32
            )

        return lax.cond(span_seen(key_segment), output_work, lambda acc: acc, total_acc)

    zero_rows = jnp.zeros((row_count, head_count, HEAD_DIM), jnp.float32)
    attended = (
        lax.fori_loop(0, span_count, output_step, zero_rows)
        .reshape(row_count, full_width)
        .astype(jnp.bfloat16)
    )
    row_delta = jnp.sum(
        grad_heads.astype(jnp.float32) * head_split(attended).astype(jnp.float32), axis=2
    )

    def all_grad_step(block_index, loop_state):
        query_acc, term_rows = loop_state
        key_heads, value_heads, key_segment = key_slice(block_index)

        def all_work(state):
            acc, terms = state
            weights_low, grad_scores = grad_parts(
                query_heads,
                grad_heads,
                own_segment,
                log_total,
                row_delta,
                key_heads,
                value_heads,
                key_segment,
            )
            acc = acc + jnp.einsum(
                "qhk,khd->qhd", grad_scores, key_heads, preferred_element_type=jnp.float32
            )
            key_part = (
                jnp.einsum(
                    "qhk,qhd->khd", grad_scores, query_heads, preferred_element_type=jnp.float32
                )
                * scale_factor
            )
            value_part = jnp.einsum(
                "qhk,qhd->khd", weights_low, grad_heads, preferred_element_type=jnp.float32
            )
            joined = jnp.concatenate(
                [key_part.reshape(key_span, full_width), value_part.reshape(key_span, full_width)],
                axis=1,
            )
            terms = lax.dynamic_update_slice_in_dim(terms, joined, block_index * key_span, 0)
            return (acc, terms)

        return lax.cond(
            span_seen(key_segment), all_work, lambda state: state, (query_acc, term_rows)
        )

    empty_terms = jnp.zeros((key_total, 2 * full_width), jnp.float32)
    query_acc, term_rows = lax.fori_loop(0, span_count, all_grad_step, (zero_rows, empty_terms))
    grad_queries = (query_acc * scale_factor).reshape(row_count, full_width).astype(jnp.bfloat16)
    both_grads = lax.psum_scatter(
        paired_order(term_rows, shard_count, row_count), "frames", scatter_dimension=0, tiled=True
    )
    grad_keys = both_grads[:, :full_width].astype(jnp.bfloat16)
    grad_values = both_grads[:, full_width:].astype(jnp.bfloat16)
    return (attended, grad_queries, grad_keys, grad_values)


def solution(mesh):
    in_specs = (
        P(("dp", "frames"), "heads"),
        P(("dp", "frames"), "heads"),
        P(("dp", "frames"), "heads"),
        P(("dp", "frames"), "heads"),
        P(("dp", "frames")),
    )
    out_specs = (
        P(("dp", "frames"), "heads"),
        P(("dp", "frames"), "heads"),
        P(("dp", "frames"), "heads"),
        P(("dp", "frames"), "heads"),
    )
    return jax.shard_map(shards, mesh=mesh, in_specs=in_specs, out_specs=out_specs, check_vma=False)
```

profile of v0, /device:TPU:2, one launch (start us, length us, event | category | flops | bytes accessed | tf_op | source)
XLA Modules:
  0.0 419.5 jit_solution(16613321960363757819)
XLA Ops:
  11.6 30.7 %all-reduce = bf16[2560]{0:T(1024)(128)(2,1)S(1)} all-reduce(bf16[2560]{0:T(1024)(128)(2,1)S(1)} %dynamic-update-slice), channel_id=1, replica_groups=mesh['frames'=16,'heads'=4,'dp'=4] {'frames'}, use_global_device_ids=true, to_apply=%add | all-reduce | flops 2560 | bytes 10240
  46.0 10.8 %all-gather.3.cloned.1.call-done = bf16[2560,1024]{1,0:T(8,128)(2,1)} async-done(((bf16[160,1024]{1,0:T(8,128)(2,1)}), bf16[2560,1024]{1,0:T(8,128)(2,1)}) %all-gather.3.cloned.1.call-update) | async-done | bytes 5242896 | tf_op jit(solution)/shard_map/all_gather | solution.py:75
  56.8 5.8 %slice_bitcast_fusion.3 = (bf16[16,80,1024]{2,1,0:T(8,128)(2,1)}, bf16[16,80,1024]{2,1,0:T(8,128)(2,1)}) fusion(bf16[16,2,80,1024]{3,2,1,0:T(8,128)(2,1)} %bitcast.123), kind=kLoop, calls=%fused_computation.54 | loop fusion | bytes 10485760 | tf_op jit(solution)/shard_map/squeeze | solution.py:18
  62.6 37.7 %all-gather.5.cloned.1.call-done = bf16[2560,1024]{1,0:T(8,128)(2,1)} async-done(((bf16[160,1024]{1,0:T(8,128)(2,1)}), bf16[2560,1024]{1,0:T(8,128)(2,1)}) %all-gather.5.cloned.1.call-update) | async-done | bytes 5242896 | tf_op jit(solution)/shard_map/all_gather | solution.py:76
  100.3 5.8 %slice_bitcast_fusion.1 = (bf16[16,80,1024]{2,1,0:T(8,128)(2,1)}, bf16[16,80,1024]{2,1,0:T(8,128)(2,1)}) fusion(bf16[16,2,80,1024]{3,2,1,0:T(8,128)(2,1)} %bitcast.124), kind=kLoop, calls=%fused_computation.52 | loop fusion | bytes 10485760 | tf_op jit(solution)/shard_map/squeeze | solution.py:18
  106.1 3.6 rev.17
  114.0 3.1 copy.77
  117.2 3.5 rev.16
  120.7 3.0 pad_maximum_fusion.1
  125.1 3.2 copy.75
  128.3 21.3 %while.46 = (s32[]{:T(128)}, f32[160,8]{0,1:T(8,128)S(1)}, f32[160,8]{0,1:T(8,128)S(1)}, f32[2560]{0:T(1024)S(1)}, f32[]{:T(128)}, /*index=5*/f32[160]{0:T(256)S...) while((s32[]{:T(128)}, f32[160,8]{0,1:T(8,128)S(1)}, ...), condition=%wide.region_7.8_spmd, body=%wide.region_1.7_spmd.sunk | while | flops 216374400 | bytes 8574873 | solution.py:114
  130.1 3.4 conditional.6
  135.5 3.4 conditional.6
  140.8 3.4 conditional.6
  146.1 3.4 conditional.6
  149.6 20.2 %while.47 = (s32[]{:T(128)}, f32[160,8,128]{2,0,1:T(8,128)S(1)}, f32[2560]{0:T(1024)S(1)}, f32[]{:T(128)}, f32[160]{0:T(256)S(1)}, /*index=5*/bf16[2560,8,128]{2...) while((s32[]{:T(128)}, f32[160,8,128]{2,0,1:T(8,128)S(1)}, ...), condition=%wide.region_12.13_spmd, body=%wide.region_8.12_spmd.sunk | while | flops 422974080 | bytes 4479369 | solution.py:132
  151.6 3.1 conditional.7
  156.7 3.1 conditional.7
  161.7 3.1 conditional.7
  166.8 3.1 conditional.7
  170.5 9.6 %broadcast_in_dim.72 = f32[2560,2048]{0,1:T(8,128)} broadcast(f32[]{:T(128)} %constant.168.clone.1), dimensions={} | broadcast | bytes 20971524 | tf_op jit(solution)/shard_map/broadcast_in_dim | solution.py:179
  180.1 53.4 %while.48 = (s32[]{:T(128)}, f32[160,8,128]{2,0,1:T(8,128)S(1)}, f32[2560,2048]{0,1:T(8,128)}, f32[2560]{0:T(1024)S(1)}, f32[]{:T(128)}, /*index=5*/f32[160]{0:T...) while((s32[]{:T(128)}, f32[160,8,128]{2,0,1:T(8,128)S(1)}, ...), condition=%wide.region_18.19_spmd, body=%wide.region_14.18_spmd.sunk | while | flops 1059000960 | bytes 37360664 | solution.py:180
  182.1 11.4 %conditional.8 = ((f32[160,8,128]{2,0,1:T(8,128)S(1)}, f32[2560,2048]{0,1:T(8,128)})) conditional(s32[]{:T(128)} %convert_element_type.106, (f32[160,8,128]{2,0,1:T(8,128)S(1)}, f32[2560,2048]{0,1:T(8,128)}) %tuple.152, (f32[640]{0:T(1024)S(1)}, f32[160]{0:T(256)S(1)}, bf16[2560,8,128]{2,0,1:T(8,128)(2,1)}, s32[]{:T(128)}, ...), branch_computations={%region_16.16_spmd, %region_17.17_spmd} | conditional | flops 1059000320 | bytes 37355208 | solution.py:175
  195.4 11.4 %conditional.8 = ((f32[160,8,128]{2,0,1:T(8,128)S(1)}, f32[2560,2048]{0,1:T(8,128)})) conditional(s32[]{:T(128)} %convert_element_type.106, (f32[160,8,128]{2,0,1:T(8,128)S(1)}, f32[2560,2048]{0,1:T(8,128)}) %tuple.152, (f32[640]{0:T(1024)S(1)}, f32[160]{0:T(256)S(1)}, bf16[2560,8,128]{2,0,1:T(8,128)(2,1)}, s32[]{:T(128)}, ...), branch_computations={%region_16.16_spmd, %region_17.17_spmd} | conditional | flops 1059000320 | bytes 37355208 | solution.py:175
  208.7 11.5 %conditional.8 = ((f32[160,8,128]{2,0,1:T(8,128)S(1)}, f32[2560,2048]{0,1:T(8,128)})) conditional(s32[]{:T(128)} %convert_element_type.106, (f32[160,8,128]{2,0,1:T(8,128)S(1)}, f32[2560,2048]{0,1:T(8,128)}) %tuple.152, (f32[640]{0:T(1024)S(1)}, f32[160]{0:T(256)S(1)}, bf16[2560,8,128]{2,0,1:T(8,128)(2,1)}, s32[]{:T(128)}, ...), branch_computations={%region_16.16_spmd, %region_17.17_spmd} | conditional | flops 1059000320 | bytes 37355208 | solution.py:175
  222.2 11.3 %conditional.8 = ((f32[160,8,128]{2,0,1:T(8,128)S(1)}, f32[2560,2048]{0,1:T(8,128)})) conditional(s32[]{:T(128)} %convert_element_type.106, (f32[160,8,128]{2,0,1:T(8,128)S(1)}, f32[2560,2048]{0,1:T(8,128)}) %tuple.152, (f32[640]{0:T(1024)S(1)}, f32[160]{0:T(256)S(1)}, bf16[2560,8,128]{2,0,1:T(8,128)(2,1)}, s32[]{:T(128)}, ...), branch_computations={%region_16.16_spmd, %region_17.17_spmd} | conditional | flops 1059000320 | bytes 37355208 | solution.py:175
  233.5 21.3 %copy.85 = f32[2560,2048]{1,0:T(8,128)} copy(f32[2560,2048]{0,1:T(8,128)} %get-tuple-element.725) | data formatting | bytes 41943040 | tf_op jit(solution)/shard_map/while | solution.py:180
  254.9 12.2 %fusion.50 = (f32[1280,2048]{1,0:T(8,128)S(1)}, f32[1280,2048]{1,0:T(8,128)}) fusion(f32[2560,2048]{1,0:T(8,128)} %copy.85), kind=kLoop, calls=%fused_computation.71 | loop fusion | bytes 41943040 | tf_op jit(solution)/shard_map/slice | solution.py:25
  267.1 9.6 %reverse_bitcast_fusion = f32[16,1,80,2048]{3,2,0,1:T(8,128)} fusion(f32[16,80,2048]{2,1,0:T(8,128)} %bitcast.118), kind=kLoop, calls=%fused_computation.48 | loop fusion | bytes 20971520 | tf_op jit(solution)/shard_map/stack | solution.py:27
  276.7 6.1 %pad_maximum_fusion = f32[16,2,80,2048]{3,2,0,1:T(8,128)S(1)} fusion(f32[16,1,80,2048]{3,2,0,1:T(8,128)} %reverse_bitcast_fusion, f32[16,1,80,2048]{3,2,0,1:T(8,128)S(1)} %bitcast.117), kind=kLoop, calls=%fused_computation.47 | loop fusion | flops 5242880 | bytes 41943040 | tf_op jit(solution)/shard_map/stack | solution.py:27
  282.8 7.3 %copy.87 = f32[16,2,80,2048]{3,2,1,0:T(8,128)} copy(f32[16,2,80,2048]{3,2,0,1:T(8,128)S(1)} %pad_maximum_fusion) | data formatting | bytes 41943040 | tf_op jit(solution)/shard_map/stack | solution.py:27
  291.8 118.9 %reduce-scatter.2.cloned.1.call-done = f32[160,2048]{1,0:T(8,128)} async-done(((f32[2560,2048]{1,0:T(8,128)}), f32[160,2048]{1,0:T(8,128)}) %reduce-scatter.2.cloned.1.call-update) | async-done | bytes 1310736 | tf_op jit(solution)/shard_map/reduce_scatter | solution.py:182
  (109 shorter events, 96.8 us)
Async XLA Ops:
  7.2 37.7 %copy-start = (bf16[160,1024]{1,0:T(8,128)(2,1)S(1)}, bf16[160,1024]{1,0:T(8,128)(2,1)}, u32[]{:S(2)}) copy-start(bf16[160,1024]{1,0:T(8,128)(2,1)} %param.17) | copy-start | bytes 983044
  7.2 49.6 %all-gather.3.cloned.1.call-start = ((), (), s32[]{:S(2)}) async-start(), calls=%async_computation.1 | async-start | bytes 5570560 | tf_op jit(solution)/shard_map/all_gather | solution.py:75
  7.9 92.4 %all-gather.5.cloned.1.call-start = ((), (), s32[]{:S(2)}) async-start(), calls=%async_computation.2 | async-start | bytes 5570560 | tf_op jit(solution)/shard_map/all_gather | solution.py:76
  8.7 402.1 %reduce-scatter.2.cloned.1.call-start = ((), (), s32[]{:S(2)}) async-start(), calls=%async_computation.3 | async-start | bytes 22282240 | tf_op jit(solution)/shard_map/reduce_scatter | solution.py:182
  290.2 122.8 %copy-start.1 = (bf16[160,1024]{1,0:T(8,128)(2,1)S(1)}, bf16[160,1024]{1,0:T(8,128)(2,1)}, u32[]{:S(2)}) copy-start(bf16[160,1024]{1,0:T(8,128)(2,1)} %param.17) | copy-start | bytes 983044
Sparse Core Ops, SparseCore 0:
  9.8 46.8 all-gather.2
  58.6 41.6 all-gather.4
  290.3 120.3 reduce-scatter.1
where the time goes:
time: 421 us; the launch traced here: 420 us
  waiting for transfers between devices  169 us (40%)
  local copies, waits for them, and re-layouts  93.6 us (22%)
  matrix products  54.1 us (13%)
  other arithmetic  41.9 us (10%)
  blocking collectives  30.7 us (7%)
  loops' own time  15.8 us (4%)
  between operations  14.5 us (3%)
    reduce_scatter x1, waiting for transfers between devices, shards(): lax.psum_scatter(paired_order(term_rows, shard_count, row_count), 'frames...  119 us
    all_gather x1, waiting for transfers between devices, shards(): lax.all_gather(values, 'frames', axis=0, tiled=True)  37.7 us
    unnamed x1, blocking collectives  30.7 us
    while x3, local copies, waits for them, and re-layouts, shards(): lax.fori_loop(0, span_count, all_grad_step, (zero_rows, empty_terms))  22.5 us
    another operation x2, local copies, waits for them, and re-layouts, paired_order(): jnp.stack([lower, upper], axis=1)  16.9 us
    dot_general x8, matrix products, score_block(): jnp.einsum('qhd,khd->qhk', query_heads, key_heads, preferred_element_type...  16.4 us
    slice x1, local copies, waits for them, and re-layouts, paired_order(): lower = parts[:shard_count]  12.2 us
    dot_general x4, matrix products, grad_parts(): jnp.einsum('qhd,khd->qhk', grad_heads, value_heads, preferred_element_typ...  11.7 us
  transfers between devices with their start and end apart: 3, of which 3 were waited for; matrix products, arithmetic and copies ran while one was open for 3% of the time, Pallas kernels for 0%

commit v1 on v0

v1 whole, which is shorter than its diff:
```python
import functools
import math

import jax
import jax.numpy as jnp
from jax import lax
from jax.experimental import pallas as pl
from jax.experimental.pallas import tpu as pltpu
from jax.sharding import PartitionSpec as P

HEAD_DIM = 128
MESH = pl.DeviceIdType.MESH
ROWS = 160
CHIPS = 8
OWN = CHIPS * ROWS
ALL = 2 * OWN
RB = 256
KC = 512
HIDDEN = -float(2**30)
SCALE = 1.0 / math.sqrt(HEAD_DIM)
SCALE2 = SCALE * math.log2(math.e)
ORDER = (4, 3, 5, 2, 6, 1, 7)
F32, BF16 = jnp.float32, jnp.bfloat16


def dot_rows(a, b):
    return lax.dot_general(a, b, (((1,), (1,)), ((), ())), preferred_element_type=F32)


def dot_plain(a, b):
    return lax.dot_general(a, b, (((1,), (0,)), ((), ())), preferred_element_type=F32)


def kernel(
    q_ref, k_ref, v_ref, g_ref, seg_ref,
    o_out, dq_out, dk_out, dv_out,
    qb, kb, vb, gb, segown, segb, eb, ab, db, vt, kt, sb, pb, inv, obuf, gn, qn,
    keep, give, got, dqb, dkb, dvb,
    in_send, in_recv, loc, fw_send, fw_recv, out_send, out_recv, out_loc, x_send, x_recv,
):
    me = lax.axis_index("frames")
    z, c = me // 2, lax.rem(me, 2)
    other = z * 2 + 1 - c

    def peer(d):
        return lax.rem(z + d, CHIPS)

    def cols(i):
        return pl.ds(pl.multiple_of(i * HEAD_DIM, HEAD_DIM), HEAD_DIM)

    def rows(i):
        return pl.ds(pl.multiple_of(i * ROWS, ROWS), ROWS)

    def krows(core, i):
        return pl.ds(pl.multiple_of((core * CHIPS + i) * ROWS, ROWS), ROWS)

    segown[:, :ROWS] = jnp.broadcast_to(seg_ref[...].astype(F32), (8, ROWS))
    segown[:, ROWS:] = jnp.zeros((8, 2 * HEAD_DIM - ROWS), F32)

    barrier = pltpu.get_barrier_semaphore()
    for d in ORDER:
        pl.semaphore_signal(barrier, inc=1, device_id={"frames": peer(d) * 2 + c}, device_id_type=MESH)
    pl.semaphore_signal(barrier, inc=1, device_id={"frames": other}, device_id_type=MESH)
    pl.semaphore_wait(barrier, CHIPS)

    def parts(a, head, source):
        if a == 4:
            return segown, segb.at[c, source]
        ref, buf = ((k_ref, kb), (q_ref, qb), (v_ref, vb), (g_ref, gb))[a]
        where = krows(c, source) if a in (0, 2) else rows(source)
        return ref.at[:, cols(head)], buf.at[where]

    def in_copy(a, d):
        src, dst = parts(a, peer(d), z)
        return pltpu.make_async_remote_copy(
            src, dst, in_send.at[a, d], in_recv.at[a, d],
            device_id={"frames": peer(d) * 2 + c}, device_id_type=MESH)

    def in_arrival(a, d):
        src, dst = parts(a, z, lax.rem(z + CHIPS - d, CHIPS))
        return pltpu.make_async_remote_copy(
            src, dst, in_send.at[a, d], in_recv.at[a, d],
            device_id={"frames": peer(d) * 2 + c}, device_id_type=MESH)

    def own_copy(a):
        src, dst = parts(a, z, z)
        return pltpu.make_async_copy(src, dst, loc.at[a])

    for a in (4, 0, 1, 2, 3):
        own_copy(a).start()
        for d in ORDER:
            in_copy(a, d).start()

    def landed(a):
        own_copy(a).wait()
        for d in ORDER:
            in_arrival(a, d).wait_recv()

    def forward(a, d):
        buf = kb if a == 0 else vb
        where = krows(c, lax.rem(z + CHIPS - d, CHIPS))
        return pltpu.make_async_remote_copy(
            buf.at[where], buf.at[where], fw_send.at[a, d], fw_recv.at[a, d],
            device_id={"frames": other}, device_id_type=MESH)

    def forwarded(a, d):
        buf = kb if a == 0 else vb
        where = krows(1 - c, lax.rem(z + CHIPS - d, CHIPS))
        return pltpu.make_async_remote_copy(
            buf.at[where], buf.at[where], fw_send.at[a, d], fw_recv.at[a, d],
            device_id={"frames": other}, device_id_type=MESH)

    def share(a):
        own_copy(a).wait()
        forward(a, 0).start()
        for d in (1, 7, 2, 6, 3, 5, 4):
            in_arrival(a, d).wait_recv()
            forward(a, d).start()

    landed(4)
    seg_fw = pltpu.make_async_remote_copy(
        segb.at[c], segb.at[c], fw_send.at[1, 0], fw_recv.at[1, 0],
        device_id={"frames": other}, device_id_type=MESH)
    seg_fw.start()
    lane = lax.broadcasted_iota(jnp.int32, (ROWS, HEAD_DIM), 1).astype(F32)

    def segment_rows(core, i):
        row = segb[core, i][0:1, :]
        return jnp.transpose(jnp.broadcast_to(row, (HEAD_DIM, 2 * HEAD_DIM)))[:ROWS]

    def own_rows(i, _):
        seg = segment_rows(c, i)
        eb[krows(c, i), :] = jnp.where(seg == lane, 1.0, 0.0).astype(BF16)
        ab[rows(i), :] = jnp.where(lane > seg, HIDDEN, 0.0).astype(BF16)
        return 0

    lax.fori_loop(0, CHIPS, own_rows, 0)
    seg_fw.wait_send()
    pltpu.make_async_remote_copy(
        segb.at[1 - c], segb.at[1 - c], fw_send.at[1, 0], fw_recv.at[1, 0],
        device_id={"frames": other}, device_id_type=MESH).wait_recv()

    def other_rows(i, _):
        eb[krows(1 - c, i), :] = jnp.where(segment_rows(1 - c, i) == lane, 1.0, 0.0).astype(BF16)
        return 0

    lax.fori_loop(0, CHIPS, other_rows, 0)

    share(0)
    landed(1)
    for d in range(CHIPS):
        forwarded(0, d).wait_recv()
    for i in range(ALL // KC):
        kt[:, i * KC : (i + 1) * KC] = jnp.transpose(kb[i * KC : (i + 1) * KC, :].astype(F32)).astype(BF16)

    def block(i):
        return pl.ds(pl.multiple_of(i * RB, RB), RB)

    def weights_step(i, _):
        qx = jnp.concatenate([qb[block(i), :], ab[block(i), :]], axis=1)
        most = jnp.full((8, RB), -jnp.inf, F32)
        for j in range(ALL // KC):
            at = slice(j * KC, (j + 1) * KC)
            kx = jnp.concatenate([kb[at, :], eb[at, :]], axis=1)
            s = dot_rows(kx, qx)
            sb[at, :] = s
            most = jnp.maximum(most, jnp.max(s.reshape(KC // 8, 8, RB), axis=0))
        top = jnp.max(most, axis=0, keepdims=True) * SCALE2
        for j in range(ALL // KC):
            at = slice(j * KC, (j + 1) * KC)
            pb[i, at, :] = jnp.exp2(sb[at, :] * SCALE2 - top).astype(BF16)
        return 0

    lax.fori_loop(0, OWN // RB, weights_step, 0)

    share(2)
    for d in range(CHIPS):
        forwarded(2, d).wait_recv()
    vt[HEAD_DIM:, :] = jnp.ones((HEAD_DIM, ALL), BF16)
    for i in range(ALL // KC):
        vt[:HEAD_DIM, i * KC : (i + 1) * KC] = jnp.transpose(vb[i * KC : (i + 1) * KC, :].astype(F32)).astype(BF16)

    def output_step(i, _):
        both = jnp.transpose(dot_plain(vt[...], pb[i]))
        part = 1.0 / both[:, HEAD_DIM:]
        inv[block(i), :] = part
        obuf[block(i), :] = (both[:, :HEAD_DIM] * part).astype(BF16)
        return 0

    lax.fori_loop(0, OWN // RB, output_step, 0)

    outs = ((obuf, o_out), (dvb, dv_out), (dqb, dq_out), (dkb, dk_out))

    def out_copy(a, d):
        buf, out = outs[a]
        return pltpu.make_async_remote_copy(
            buf.at[rows(peer(d))], out.at[:, cols(z)], out_send.at[a, d], out_recv.at[a, d],
            device_id={"frames": peer(d) * 2 + c}, device_id_type=MESH)

    def out_arrival(a, d):
        buf, out = outs[a]
        source = lax.rem(z + CHIPS - d, CHIPS)
        return pltpu.make_async_remote_copy(
            buf.at[rows(source)], out.at[:, cols(source)], out_send.at[a, d], out_recv.at[a, d],
            device_id={"frames": peer(d) * 2 + c}, device_id_type=MESH)

    def out_own(a):
        buf, out = outs[a]
        return pltpu.make_async_copy(buf.at[rows(z)], out.at[:, cols(z)], out_loc.at[a])

    def send_back(a):
        for d in ORDER:
            out_copy(a, d).start()
        out_own(a).start()

    send_back(0)

    landed(3)
    narrow = lax.broadcasted_iota(jnp.int32, (RB, HEAD_DIM), 1)

    def delta_step(i, _):
        g = gb[block(i), :].astype(F32)
        part = inv[block(i), :]
        gn[block(i), :] = (g * part).astype(BF16)
        qn[block(i), :] = (qb[block(i), :].astype(F32) * (part * SCALE)).astype(BF16)
        delta = -jnp.sum(g * obuf[block(i), :].astype(F32), axis=1, keepdims=True)
        first = delta.astype(BF16).astype(F32)
        second = (delta - first).astype(BF16).astype(F32)
        third = delta - first - second
        cells = jnp.where(narrow == 0, first, jnp.where(narrow == 1, second, jnp.where(narrow == 2, third, 0.0)))
        db[block(i), :] = cells.astype(BF16)
        return 0

    lax.fori_loop(0, OWN // RB, delta_step, 0)

    def key_sums(right, a, result):
        def terms(core, j):
            at = pl.ds(pl.multiple_of(core * OWN + j * RB, RB), RB)
            total = dot_plain(pb[0, at, :], right[0:RB, :])
            for i in range(1, OWN // RB):
                total = total + dot_plain(pb[i, at, :], right[i * RB : (i + 1) * RB, :])
            return total

        def swap(j):
            at = slice(j * RB, (j + 1) * RB)
            return pltpu.make_async_remote_copy(
                give.at[a, at], got.at[a, at], x_send.at[a, j], x_recv.at[a, j],
                device_id={"frames": other}, device_id_type=MESH)

        for j in range(OWN // RB):
            give[a, j * RB : (j + 1) * RB, :] = terms(1 - c, j)
            swap(j).start()

        def mine(j, _):
            keep[block(j), :] = terms(c, j)
            return 0

        lax.fori_loop(0, OWN // RB, mine, 0)
        for j in range(OWN // RB):
            at = slice(j * RB, (j + 1) * RB)
            swap(j).wait()
            result[at, :] = (keep[at, :] + got[a, at, :]).astype(BF16)

    key_sums(gn, 0, dvb)
    send_back(1)

    ones = jnp.ones((KC, HEAD_DIM), BF16)

    def grad_step(i, _):
        gx = jnp.concatenate([gb[block(i), :], db[block(i), :]], axis=1)
        for j in range(ALL // KC):
            at = slice(j * KC, (j + 1) * KC)
            vx = jnp.concatenate([vb[at, :], ones], axis=1)
            pb[i, at, :] = (pb[i, at, :].astype(F32) * dot_rows(vx, gx)).astype(BF16)
        dq = jnp.transpose(dot_plain(kt[...], pb[i]))
        dqb[block(i), :] = (dq * (inv[block(i), :] * SCALE)).astype(BF16)
        return 0

    lax.fori_loop(0, OWN // RB, grad_step, 0)
    send_back(2)
    key_sums(qn, 1, dkb)
    send_back(3)

    for a in range(5):
        for d in ORDER:
            in_copy(a, d).wait_send()
    for a in (0, 2):
        for d in range(CHIPS):
            forward(a, d).wait_send()
    for a in range(4):
        out_own(a).wait()
        for d in ORDER:
            out_copy(a, d).wait_send()
            out_arrival(a, d).wait_recv()


def shards(queries, key_vectors, values, grad_output, segment_index):
    vmem, sems = pltpu.VMEM, pltpu.SemaphoreType.DMA
    out = jax.ShapeDtypeStruct(queries.shape, BF16)
    any_spec = pl.BlockSpec(memory_space=pl.ANY)
    vmem_spec = pl.BlockSpec(memory_space=pltpu.VMEM)
    attended, grad_queries, grad_keys, grad_values = pl.pallas_call(
        kernel,
        out_shape=[out] * 4,
        in_specs=[any_spec] * 4 + [vmem_spec],
        out_specs=[OUT_SPEC] * 4,
        scratch_shapes=[
            vmem((OWN, HEAD_DIM), BF16),
            vmem((ALL, HEAD_DIM), BF16),
            vmem((ALL, HEAD_DIM), BF16),
            vmem((OWN, HEAD_DIM), BF16),
            vmem((8, 2 * HEAD_DIM), F32),
            vmem((2, CHIPS, 8, 2 * HEAD_DIM), F32),
            vmem((ALL, HEAD_DIM), BF16),
            vmem((OWN, HEAD_DIM), BF16),
            vmem((OWN, HEAD_DIM), BF16),
            vmem((2 * HEAD_DIM, ALL), BF16),
            vmem((HEAD_DIM, ALL), BF16),
            vmem((ALL, RB), F32),
            vmem((OWN // RB, ALL, RB), BF16),
            vmem((OWN, HEAD_DIM), F32),
            vmem((OWN, HEAD_DIM), BF16),
            vmem((OWN, HEAD_DIM), BF16),
            vmem((OWN, HEAD_DIM), BF16),
            vmem((OWN, HEAD_DIM), F32),
            vmem((2, OWN, HEAD_DIM), F32),
            vmem((2, OWN, HEAD_DIM), F32),
            vmem((OWN, HEAD_DIM), BF16),
            vmem((OWN, HEAD_DIM), BF16),
            vmem((OWN, HEAD_DIM), BF16),
            sems((5, CHIPS)),
            sems((5, CHIPS)),
            sems((5,)),
            sems((3, CHIPS)),
            sems((3, CHIPS)),
            sems((4, CHIPS)),
            sems((4, CHIPS)),
            sems((4,)),
            sems((2, OWN // RB)),
            sems((2, OWN // RB)),
        ],
        compiler_params=pltpu.CompilerParams(
            collective_id=0, has_side_effects=True, vmem_limit_bytes=56 << 20
        ),
        cost_estimate=pl.CostEstimate(
            flops=12 * OWN * ALL * HEAD_DIM, bytes_accessed=8 * ROWS * 1024 * 2, transcendentals=OWN * ALL
        ),
    )(queries, key_vectors, values, grad_output, segment_index.reshape(1, ROWS))
    return (attended, grad_queries, grad_keys, grad_values)


OUT_SPEC = pl.BlockSpec(memory_space=pl.ANY)


def solution(mesh):
    wide = P(("dp", "frames"), "heads")
    return jax.shard_map(
        shards,
        mesh=mesh,
        in_specs=(wide, wide, wide, wide, P(("dp", "frames"))),
        out_specs=(wide, wide, wide, wide),
        check_vma=False,
    )
```

time: 421 us -> 76.9 us (0.18)
  waiting for transfers between devices: 169 us -> 0 us
  local copies, waits for them, and re-layouts: 93.6 us -> 4.67 us
  Pallas kernels: 0 us -> 70.3 us
  matrix products: 54.1 us -> 0 us
  other arithmetic: 41.9 us -> 0 us
  blocking collectives: 30.7 us -> 0 us
  loops' own time: 15.8 us -> 0 us
  between operations: 14.5 us -> 0.65 us
    reduce_scatter x1 -> x0, waiting for transfers between devices: 119 us -> none  [shards(): lax.psum_scatter(paired_order(term_rows, shard_count, row_count), 'frames...]
    pallas_call x0 -> x1, Pallas kernels: none -> 70.3 us  [shards(): pl.pallas_call(kernel, out_shape=[out] * 4, in_specs=[any_spec] * 4 + [vm...]
    dot_general x28 -> x0, matrix products: 54.1 us -> none  [the longest x8 16.4 us: score_block(): jnp.einsum('qhd,khd->qhk', query_heads, key_heads, preferred_element_type...]
    all_gather x2 -> x0, waiting for transfers between devices: 48.5 us -> none  [the longest x1 37.7 us: shards(): lax.all_gather(values, 'frames', axis=0, tiled=True)]
    unnamed x1 -> x0, blocking collectives: 30.7 us -> none
    while x5 -> x0, local copies, waits for them, and re-layouts: 28.8 us -> none  [the longest x3 22.5 us: shards(): lax.fori_loop(0, span_count, all_grad_step, (zero_rows, empty_terms))]
    another operation x2 -> x0, local copies, waits for them, and re-layouts: 16.9 us -> none  [paired_order(): jnp.stack([lower, upper], axis=1)]
    another operation x15 -> x0, loops' own time: 15.8 us -> none  [the longest x1 5.2 us: shards(): lax.fori_loop(0, span_count, output_step, zero_rows)]
  transfers between devices with their start and end apart: 3 -> 0, of which waited for: 3 -> 0; matrix products, arithmetic and copies ran while one was open for 3% -> 0% of each run, Pallas kernels for 0% -> 0%
where the time goes in v1:
time: 76.9 us; the launch traced here: 75.6 us
  Pallas kernels  70.3 us (91%)
  local copies, waits for them, and re-layouts  4.67 us (6%)
    pallas_call x1, Pallas kernels, shards(): pl.pallas_call(kernel, out_shape=[out] * 4, in_specs=[any_spec] * 4 + [vm...  70.3 us
    unnamed x10, local copies, waits for them, and re-layouts  4.67 us

profile of v1, /device:TPU:2, one launch (start us, length us, event | category | flops | bytes accessed | tf_op | source)
XLA Modules:
  0.0 75.6 jit_solution(5918452838622291305)
XLA Ops:
  0.6 70.3 %shard_map.84 = (bf16[160,1024]{1,0:T(8,128)(2,1)}, bf16[160,1024]{1,0:T(8,128)(2,1)}, bf16[160,1024]{1,0:T(8,128)(2,1)}, bf16[160,1024]{1,0:T(8,128)(2,1)}) custom-call(bf16[160,1024]{1,0:T(8,128)(2,1)} %q_ref.1, bf16[160,1024]{1,0:T(8,128)(2,1)} %k_ref.1, bf16[160,1024]{1,0:T(8,128)(2,1)} %v_ref.1, bf16[160,1024]{1,0:T(8,128)(2,1)} %g_ref.1, s32[1,160]{1,0:T(1,128)} %bitcast.1), custom_call_target="tpu_custom_call" | custom-call | flops 5033164800 | bytes 2621440 | tf_op jit(solution)/shard_map/pallas_call | solution.py:302
  70.9 0.0 copy-start.2
  70.9 1.8 %copy.13 = bf16[160,1024]{1,0:T(8,128)(2,1)} copy(bf16[160,1024]{1,0:T(8,128)(2,1)} %get-tuple-element.8) | data formatting | bytes 655360
  72.7 0.0 copy-done.2
  72.7 0.0 copy-start.1
  72.7 0.7 copy.14
  73.4 0.4 copy-done.1
  73.8 0.0 copy-start
  73.8 0.7 copy.15
  74.5 0.4 copy-done
  74.9 0.7 copy.16
Async XLA Ops:
  70.9 1.8 %copy-start.2 = (bf16[160,1024]{1,0:T(8,128)(2,1)S(1)}, bf16[160,1024]{1,0:T(8,128)(2,1)}, u32[]{:S(2)}) copy-start(bf16[160,1024]{1,0:T(8,128)(2,1)} %get-tuple-element.9) | copy-start | bytes 983044
  72.7 1.1 %copy-start.1 = (bf16[160,1024]{1,0:T(8,128)(2,1)S(1)}, bf16[160,1024]{1,0:T(8,128)(2,1)}, u32[]{:S(2)}) copy-start(bf16[160,1024]{1,0:T(8,128)(2,1)} %get-tuple-element.10) | copy-start | bytes 983044
  73.8 1.1 %copy-start = (bf16[160,1024]{1,0:T(8,128)(2,1)S(1)}, bf16[160,1024]{1,0:T(8,128)(2,1)}, u32[]{:S(2)}) copy-start(bf16[160,1024]{1,0:T(8,128)(2,1)} %get-tuple-element.11) | copy-start | bytes 983044

commit v2 on v1

v2 whole, which is shorter than its diff:
```python
import functools
import math

import jax
import jax.numpy as jnp
from jax import lax
from jax.experimental import pallas as pl
from jax.experimental.pallas import tpu as pltpu
from jax.sharding import PartitionSpec as P

HEAD_DIM = 128
MESH = pl.DeviceIdType.MESH
ROWS = 160
CHIPS = 8
OWN = CHIPS * ROWS
ALL = 2 * OWN
RB = 256
KC = 512
HIDDEN = -float(2**30)
SCALE = 1.0 / math.sqrt(HEAD_DIM)
SCALE2 = SCALE * math.log2(math.e)
PIECE = RB // CHIPS
BLOCKS = OWN // RB
GROUPS = ((0, 2), (2, 5))
ORDER = ((4, 4), (3, 5), (5, 3), (2, 6), (6, 2), (1, 7), (7, 1))
F32, BF16 = jnp.float32, jnp.bfloat16


def dot_rows(a, b):
    return lax.dot_general(a, b, (((1,), (1,)), ((), ())), preferred_element_type=F32)


def dot_plain(a, b):
    return lax.dot_general(a, b, (((1,), (0,)), ((), ())), preferred_element_type=F32)


def kernel(
    q_ref, k_ref, v_ref, g_ref, seg_ref,
    o_out, dq_out, dk_out, dv_out,
    qb, kb, vb, gb, segin, segown, segb, eb, ab, vt, kt, sb, pb, ds, inv, obuf, gn, qn,
    give, got, dqb, dkb, dvb,
    seg_sem, in_send, in_recv, loc, g_send, g_recv, g_loc, fw_send, fw_recv, out_send, out_recv, out_loc, x_send, x_recv,
):
    me = lax.axis_index("frames")
    z, c = me // 2, lax.rem(me, 2)
    other = z * 2 + 1 - c

    def peer(d):
        return lax.rem(z + d, CHIPS)

    def cols(i):
        return pl.ds(pl.multiple_of(i * HEAD_DIM, HEAD_DIM), HEAD_DIM)

    def rows(i):
        return pl.ds(pl.multiple_of(i * ROWS, ROWS), ROWS)

    def krows(core, i):
        return pl.ds(pl.multiple_of((core * CHIPS + i) * ROWS, ROWS), ROWS)

    seg_copy = pltpu.make_async_copy(seg_ref, segin, seg_sem)
    seg_copy.start()

    barrier = pltpu.get_barrier_semaphore()
    for d in range(1, CHIPS):
        pl.semaphore_signal(barrier, inc=1, device_id={"frames": peer(d) * 2 + c}, device_id_type=MESH)
    pl.semaphore_signal(barrier, inc=1, device_id={"frames": other}, device_id_type=MESH)
    seg_copy.wait()
    segown[:, :ROWS] = jnp.broadcast_to(segin[...].astype(F32), (8, ROWS))
    segown[:, ROWS:] = jnp.zeros((8, 2 * HEAD_DIM - ROWS), F32)
    pl.semaphore_wait(barrier, CHIPS)

    def parts(a, head, source):
        if a == 4:
            return segown, segb.at[c, source]
        if a == 1:
            return q_ref.at[:, :, cols(head)], qb.at[:, source]
        ref, buf = (k_ref, kb) if a == 0 else (v_ref, vb)
        return ref.at[:, cols(head)], buf.at[krows(c, source)]

    def in_copy(a, d):
        src, dst = parts(a, peer(d), z)
        return pltpu.make_async_remote_copy(
            src, dst, in_send.at[a, d], in_recv.at[a, d],
            device_id={"frames": peer(d) * 2 + c}, device_id_type=MESH)

    def in_arrival(a, d):
        src, dst = parts(a, z, lax.rem(z + CHIPS - d, CHIPS))
        return pltpu.make_async_remote_copy(
            src, dst, in_send.at[a, d], in_recv.at[a, d],
            device_id={"frames": peer(d) * 2 + c}, device_id_type=MESH)

    def own_copy(a):
        src, dst = parts(a, z, z)
        return pltpu.make_async_copy(src, dst, loc.at[a])

    def g_parts(group, head, source):
        span = pl.ds(GROUPS[group][0], GROUPS[group][1] - GROUPS[group][0])
        return g_ref.at[span, :, cols(head)], gb.at[span, source]

    def g_copy(group, d, head, source):
        src, dst = g_parts(group, head, source)
        return pltpu.make_async_remote_copy(
            src, dst, g_send.at[group, d], g_recv.at[group, d],
            device_id={"frames": peer(d) * 2 + c}, device_id_type=MESH)

    def g_own(group):
        src, dst = g_parts(group, z, z)
        return pltpu.make_async_copy(src, dst, g_loc.at[group])

    turns = [a if a == b else jnp.where(c == 0, a, b) for a, b in ORDER]
    for a in (4, 0, 1, 2):
        for d in turns:
            in_copy(a, d).start()
        own_copy(a).start()
    for group in range(len(GROUPS)):
        for d in turns:
            g_copy(group, d, peer(d), z).start()
        g_own(group).start()

    def landed(a):
        own_copy(a).wait()
        for d in range(1, CHIPS):
            in_arrival(a, d).wait_recv()

    def forward(a, d):
        buf = kb if a == 0 else vb
        where = krows(c, lax.rem(z + CHIPS - d, CHIPS))
        return pltpu.make_async_remote_copy(
            buf.at[where], buf.at[where], fw_send.at[a, d], fw_recv.at[a, d],
            device_id={"frames": other}, device_id_type=MESH)

    def forwarded(a, d):
        buf = kb if a == 0 else vb
        where = krows(1 - c, lax.rem(z + CHIPS - d, CHIPS))
        return pltpu.make_async_remote_copy(
            buf.at[where], buf.at[where], fw_send.at[a, d], fw_recv.at[a, d],
            device_id={"frames": other}, device_id_type=MESH)

    def share(a):
        own_copy(a).wait()
        forward(a, 0).start()
        for d in (1, 7, 2, 6, 3, 5, 4):
            in_arrival(a, d).wait_recv()
            forward(a, d).start()

    landed(4)
    seg_fw = pltpu.make_async_remote_copy(
        segb.at[c], segb.at[c], fw_send.at[1, 0], fw_recv.at[1, 0],
        device_id={"frames": other}, device_id_type=MESH)
    seg_fw.start()
    lane = lax.broadcasted_iota(jnp.int32, (ROWS, HEAD_DIM), 1).astype(F32)

    def segment_rows(core, i):
        row = segb[core, i][0:1, :]
        return jnp.transpose(jnp.broadcast_to(row, (HEAD_DIM, 2 * HEAD_DIM)))[:ROWS]

    def own_rows(i, _):
        seg = segment_rows(c, i)
        eb[krows(c, i), :] = jnp.where(seg == lane, 1.0, 0.0).astype(BF16)
        hiding = jnp.where(lane > seg, HIDDEN, 0.0).astype(BF16)
        for j in range(BLOCKS):
            ab[j, i] = hiding[j * PIECE : (j + 1) * PIECE]
        return 0

    lax.fori_loop(0, CHIPS, own_rows, 0)
    seg_fw.wait_send()
    pltpu.make_async_remote_copy(
        segb.at[1 - c], segb.at[1 - c], fw_send.at[1, 0], fw_recv.at[1, 0],
        device_id={"frames": other}, device_id_type=MESH).wait_recv()

    def other_rows(i, _):
        eb[krows(1 - c, i), :] = jnp.where(segment_rows(1 - c, i) == lane, 1.0, 0.0).astype(BF16)
        return 0

    lax.fori_loop(0, CHIPS, other_rows, 0)

    share(0)
    landed(1)
    for d in range(CHIPS):
        forwarded(0, d).wait_recv()
    for i in range(ALL // KC):
        kt[:, i * KC : (i + 1) * KC] = jnp.transpose(kb[i * KC : (i + 1) * KC, :].astype(F32)).astype(BF16)

    def flat(ref, i):
        return ref[i].reshape(RB, HEAD_DIM)

    def pieces(array):
        return array.reshape(CHIPS, PIECE, HEAD_DIM)

    def block(i):
        return pl.ds(pl.multiple_of(i * RB, RB), RB)

    def weights_step(i, _):
        qx = jnp.concatenate([flat(qb, i), flat(ab, i)], axis=1)
        most = jnp.full((8, RB), -jnp.inf, F32)
        for j in range(ALL // KC):
            at = slice(j * KC, (j + 1) * KC)
            kx = jnp.concatenate([kb[at, :], eb[at, :]], axis=1)
            s = dot_rows(kx, qx)
            sb[at, :] = s
            most = jnp.maximum(most, jnp.max(s.reshape(KC // 8, 8, RB), axis=0))
        top = jnp.max(most, axis=0, keepdims=True) * SCALE2
        for j in range(ALL // KC):
            at = slice(j * KC, (j + 1) * KC)
            pb[i, at, :] = jnp.exp2(sb[at, :] * SCALE2 - top).astype(BF16)
        return 0

    lax.fori_loop(0, OWN // RB, weights_step, 0)

    share(2)
    for d in range(CHIPS):
        forwarded(2, d).wait_recv()
    vt[HEAD_DIM:, :] = jnp.ones((HEAD_DIM, ALL), BF16)
    for i in range(ALL // KC):
        vt[:HEAD_DIM, i * KC : (i + 1) * KC] = jnp.transpose(vb[i * KC : (i + 1) * KC, :].astype(F32)).astype(BF16)

    def output_step(i, _):
        both = jnp.transpose(dot_plain(vt[...], pb[i]))
        part = 1.0 / both[:, HEAD_DIM:]
        inv[block(i), :] = part
        obuf[i] = pieces((both[:, :HEAD_DIM] * part).astype(BF16))
        return 0

    lax.fori_loop(0, OWN // RB, output_step, 0)

    def back(a, to, source):
        if a == 0:
            return obuf.at[:, to], o_out.at[:, :, cols(source)]
        if a < 3:
            buf, out = ((dvb, dv_out), (dkb, dk_out))[a - 1]
            return buf.at[rows(to)], out.at[:, cols(source)]
        low, high = GROUPS[a - 3]
        span = pl.ds(low, high - low)
        return dqb.at[span, to], dq_out.at[span, :, cols(source)]

    def out_copy(a, d):
        src, dst = back(a, peer(d), z)
        return pltpu.make_async_remote_copy(
            src, dst, out_send.at[a, d], out_recv.at[a, d],
            device_id={"frames": peer(d) * 2 + c}, device_id_type=MESH)

    def out_arrival(a, d):
        source = lax.rem(z + CHIPS - d, CHIPS)
        src, dst = back(a, source, source)
        return pltpu.make_async_remote_copy(
            src, dst, out_send.at[a, d], out_recv.at[a, d],
            device_id={"frames": peer(d) * 2 + c}, device_id_type=MESH)

    def out_own(a):
        src, dst = back(a, z, z)
        return pltpu.make_async_copy(src, dst, out_loc.at[a])

    def send_back(a):
        for d in turns:
            out_copy(a, d).start()
        out_own(a).start()

    send_back(0)

    narrow = lax.broadcasted_iota(jnp.int32, (RB, HEAD_DIM), 1)
    ones = jnp.ones((KC, HEAD_DIM), BF16)

    def grad_step(i, _):
        low = flat(gb, i)
        g = low.astype(F32)
        part = inv[block(i), :]
        gn[block(i), :] = (g * part).astype(BF16)
        qn[block(i), :] = (flat(qb, i).astype(F32) * (part * SCALE)).astype(BF16)
        delta = -jnp.sum(g * flat(obuf, i).astype(F32), axis=1, keepdims=True)
        first = delta.astype(BF16).astype(F32)
        second = (delta - first).astype(BF16).astype(F32)
        third = delta - first - second
        cells = jnp.where(narrow == 0, first, jnp.where(narrow == 1, second, jnp.where(narrow == 2, third, 0.0)))
        gx = jnp.concatenate([low, cells.astype(BF16)], axis=1)
        for j in range(ALL // KC):
            at = slice(j * KC, (j + 1) * KC)
            vx = jnp.concatenate([vb[at, :], ones], axis=1)
            ds[i, at, :] = (pb[i, at, :].astype(F32) * dot_rows(vx, gx)).astype(BF16)
        dq = jnp.transpose(dot_plain(kt[...], ds[i]))
        dqb[i] = pieces((dq * (part * SCALE)).astype(BF16))
        return 0

    for group, (low, high) in enumerate(GROUPS):
        g_own(group).wait()
        for d in range(1, CHIPS):
            g_copy(group, d, z, lax.rem(z + CHIPS - d, CHIPS)).wait_recv()
        lax.fori_loop(low, high, grad_step, 0)
        send_back(3 + group)

    def terms(left, right, core, j):
        at = pl.ds(pl.multiple_of(core * OWN + j * RB, RB), RB)
        total = dot_plain(left[0, at, :], right[0:RB, :])
        for i in range(1, BLOCKS):
            total = total + dot_plain(left[i, at, :], right[i * RB : (i + 1) * RB, :])
        return total

    def swap(a, j):
        at = slice(j * RB, (j + 1) * RB)
        return pltpu.make_async_remote_copy(
            give.at[a, at], got.at[a, at], x_send.at[a, j], x_recv.at[a, j],
            device_id={"frames": other}, device_id_type=MESH)

    sums = ((pb, gn, dvb), (ds, qn, dkb))
    for a, (left, right, _) in enumerate(sums):
        for j in range(BLOCKS):
            give[a, j * RB : (j + 1) * RB, :] = terms(left, right, 1 - c, j)
            swap(a, j).start()
    for a, (left, right, result) in enumerate(sums):
        for j in range(BLOCKS):
            mine = terms(left, right, c, j)
            swap(a, j).wait()
            at = slice(j * RB, (j + 1) * RB)
            result[at, :] = (mine + got[a, at, :]).astype(BF16)
        send_back(1 + a)

    for d in range(1, CHIPS):
        for a in (4, 0, 1, 2):
            in_copy(a, d).wait_send()
        for group in range(len(GROUPS)):
            g_copy(group, d, peer(d), z).wait_send()
    for a in (0, 2):
        for d in range(CHIPS):
            forward(a, d).wait_send()
    for a in range(3 + len(GROUPS)):
        out_own(a).wait()
        for d in range(1, CHIPS):
            out_copy(a, d).wait_send()
            out_arrival(a, d).wait_recv()


def shards(queries, key_vectors, values, grad_output, segment_index):
    vmem, sems = pltpu.VMEM, pltpu.SemaphoreType.DMA
    any_spec = pl.BlockSpec(memory_space=pl.ANY)
    whole = jax.ShapeDtypeStruct(queries.shape, BF16)
    cut = jax.ShapeDtypeStruct((BLOCKS, PIECE, queries.shape[1]), BF16)
    by_block = (BLOCKS, CHIPS, PIECE, HEAD_DIM)
    found = pl.pallas_call(
        kernel,
        out_shape=[vmem(array.shape, BF16) for array in (cut, cut, whole, whole)],
        in_specs=[any_spec] * 5,
        out_specs=[any_spec] * 4,
        scratch_shapes=[
            vmem(by_block, BF16),
            vmem((ALL, HEAD_DIM), BF16),
            vmem((ALL, HEAD_DIM), BF16),
            vmem(by_block, BF16),
            vmem((1, ROWS), jnp.int32),
            vmem((8, 2 * HEAD_DIM), F32),
            vmem((2, CHIPS, 8, 2 * HEAD_DIM), F32),
            vmem((ALL, HEAD_DIM), BF16),
            vmem(by_block, BF16),
            vmem((2 * HEAD_DIM, ALL), BF16),
            vmem((HEAD_DIM, ALL), BF16),
            vmem((ALL, RB), F32),
            vmem((BLOCKS, ALL, RB), BF16),
            vmem((BLOCKS, ALL, RB), BF16),
            vmem((OWN, HEAD_DIM), F32),
            vmem(by_block, BF16),
            vmem((OWN, HEAD_DIM), BF16),
            vmem((OWN, HEAD_DIM), BF16),
            vmem((2, OWN, HEAD_DIM), F32),
            vmem((2, OWN, HEAD_DIM), F32),
            vmem(by_block, BF16),
            vmem((OWN, HEAD_DIM), BF16),
            vmem((OWN, HEAD_DIM), BF16),
            pltpu.SemaphoreType.DMA,
            sems((5, CHIPS)),
            sems((5, CHIPS)),
            sems((5,)),
            sems((len(GROUPS), CHIPS)),
            sems((len(GROUPS), CHIPS)),
            sems((len(GROUPS),)),
            sems((3, CHIPS)),
            sems((3, CHIPS)),
            sems((3 + len(GROUPS), CHIPS)),
            sems((3 + len(GROUPS), CHIPS)),
            sems((3 + len(GROUPS),)),
            sems((2, BLOCKS)),
            sems((2, BLOCKS)),
        ],
        compiler_params=pltpu.CompilerParams(
            collective_id=0, has_side_effects=True, vmem_limit_bytes=40 << 20
        ),
        cost_estimate=pl.CostEstimate(
            flops=12 * OWN * ALL * HEAD_DIM, bytes_accessed=8 * ROWS * 1024 * 2, transcendentals=OWN * ALL
        ),
    )(*[
        pltpu.with_memory_space_constraint(array, pltpu.HBM)
        for array in (
            queries.reshape(cut.shape), key_vectors, values, grad_output.reshape(cut.shape),
            segment_index.reshape(1, ROWS),
        )
    ])
    return pl.pallas_call(
        hand_over,
        out_shape=[whole] * 4,
        in_specs=[any_spec] * 4,
        out_specs=[any_spec] * 4,
        scratch_shapes=[sems((4,))],
    )(*[pltpu.with_memory_space_constraint(array.reshape(whole.shape), pltpu.VMEM) for array in found])


def hand_over(*refs):
    sources, outs, sem = refs[:4], refs[4:8], refs[8]
    copies = [pltpu.make_async_copy(src, out, sem.at[a]) for a, (src, out) in enumerate(zip(sources, outs))]
    for copy in copies:
        copy.start()
    for copy in copies:
        copy.wait()


def solution(mesh):
    wide = P(("dp", "frames"), "heads")
    return jax.shard_map(
        shards,
        mesh=mesh,
        in_specs=(wide, wide, wide, wide, P(("dp", "frames"))),
        out_specs=(wide, wide, wide, wide),
        check_vma=False,
    )
```

time: 76.9 us -> 72.4 us (0.941)
  local copies, waits for them, and re-layouts: 4.67 us -> 0 us
    unnamed x10 -> x0, local copies, waits for them, and re-layouts: 4.67 us -> none
    pallas_call x1 -> x2, Pallas kernels: 70.3 us -> 70.5 us  [the longest x1 69.4 us: shards(): pl.pallas_call(kernel, out_shape=[vmem(array.shape, BF16) for array in (c...]
where the time goes in v2:
time: 72.4 us; the launch traced here: 71.1 us
  Pallas kernels  70.5 us (97%)
    pallas_call x1, Pallas kernels, shards(): pl.pallas_call(kernel, out_shape=[vmem(array.shape, BF16) for array in (c...  69.4 us

profile of v2, /device:TPU:2, one launch (start us, length us, event | category | flops | bytes accessed | tf_op | source)
XLA Modules:
  0.0 71.1 jit_solution(2915601349120520950)
XLA Ops:
  0.6 69.4 %shard_map.84 = (bf16[5,32,1024]{2,1,0:T(8,128)(2,1)S(1)}, bf16[5,32,1024]{2,1,0:T(8,128)(2,1)S(1)}, bf16[160,1024]{1,0:T(8,128)(2,1)S(1)}, bf16[160,1024]{1,0:T(8,128)(2,1)S(1)}) custom-call(bf16[5,32,1024]{2,1,0:T(8,128)(2,1)} %bitcast.7, bf16[160,1024]{1,0:T(8,128)(2,1)} %k_ref.1, bf16[160,1024]{1,0:T(8,128)(2,1)} %v_ref.1, bf16[5,32,1024]{2,1,0:T(8,128)(2,1)} %bitcast.8, ...), custom_call_target="tpu_custom_call" | custom-call | flops 5033164800 | bytes 2621440 | tf_op jit(solution)/shard_map/pallas_call | solution.py:337
  70.1 1.1 %shard_map.85 = (bf16[160,1024]{1,0:T(8,128)(2,1)}, bf16[160,1024]{1,0:T(8,128)(2,1)}, bf16[160,1024]{1,0:T(8,128)(2,1)}, bf16[160,1024]{1,0:T(8,128)(2,1)}) custom-call(bf16[160,1024]{1,0:T(8,128)(2,1)S(1)} %bitcast.5, bf16[160,1024]{1,0:T(8,128)(2,1)S(1)} %bitcast.6, bf16[160,1024]{1,0:T(8,128)(2,1)S(1)} %get-tuple-element.10.refs_2_, ...), custom_call_target="tpu_custom_call" | custom-call | tf_op jit(solution)/shard_map/pallas_call | solution.py:394

commit v3 on v2

v3 whole, which is shorter than its diff:
```python
import functools
import math

import jax
import jax.numpy as jnp
from jax import lax
from jax.experimental import pallas as pl
from jax.experimental.pallas import tpu as pltpu
from jax.sharding import PartitionSpec as P

HEAD_DIM = 128
MESH = pl.DeviceIdType.MESH
ROWS = 160
CHIPS = 8
OWN = CHIPS * ROWS
ALL = 2 * OWN
RB = 256
KC = 512
HIDDEN = -float(2**30)
SCALE = 1.0 / math.sqrt(HEAD_DIM)
SCALE2 = SCALE * math.log2(math.e)
PIECE = RB // CHIPS
BLOCKS = OWN // RB
GROUPS = ((0, 0, 2), (0, 2, 5), (1, 0, 3), (1, 3, 5))
ORDER = ((4, 4), (3, 5), (5, 3), (2, 6), (6, 2), (1, 7), (7, 1))
FAR_FIRST = (4, 3, 5, 2, 6, 1, 7)
F32, BF16 = jnp.float32, jnp.bfloat16


def dot_rows(a, b):
    return lax.dot_general(a, b, (((1,), (1,)), ((), ())), preferred_element_type=F32)


def dot_plain(a, b):
    return lax.dot_general(a, b, (((1,), (0,)), ((), ())), preferred_element_type=F32)


def kernel(
    q_ref, k_ref, v_ref, g_ref, seg_ref,
    oq_out, kv_out,
    kv_in, qg_in, kvb, qgb, segin, segown, segb, eb, ab, vt, kt, sb, pb, ds, inv, gn, qn,
    give, got, oqb, kvg,
    seg_sem, stage, in_send, in_recv, loc, fw_send, fw_recv, out_send, out_recv, out_loc, x_send, x_recv,
):
    me = lax.axis_index("frames")
    z, c = me // 2, lax.rem(me, 2)
    other = {"frames": z * 2 + 1 - c}

    def peer(d):
        return lax.rem(z + d, CHIPS)

    def chip(i):
        return {"frames": i * 2 + c}

    def cols(i):
        return pl.ds(pl.multiple_of(i * HEAD_DIM, HEAD_DIM), HEAD_DIM)

    def rows(i):
        return pl.ds(pl.multiple_of(i * ROWS, ROWS), ROWS)

    def krows(core, i):
        return pl.ds(pl.multiple_of((core * CHIPS + i) * ROWS, ROWS), ROWS)

    seg_copy = pltpu.make_async_copy(seg_ref, segin, seg_sem)
    seg_copy.start()
    stages = [
        pltpu.make_async_copy(src, dst, stage.at[a])
        for a, (src, dst) in enumerate(
            ((k_ref, kv_in.at[0]), (v_ref, kv_in.at[1]), (q_ref, qg_in.at[0]), (g_ref, qg_in.at[1]))
        )
    ]
    for copy in stages:
        copy.start()

    barrier = pltpu.get_barrier_semaphore()
    for d in FAR_FIRST:
        pl.semaphore_signal(barrier, inc=1, device_id=chip(peer(d)), device_id_type=MESH)
    pl.semaphore_signal(barrier, inc=1, device_id=other, device_id_type=MESH)
    seg_copy.wait()
    segown[:, :ROWS] = jnp.broadcast_to(segin[...].astype(F32), (8, ROWS))
    segown[:, ROWS:] = jnp.zeros((8, 2 * HEAD_DIM - ROWS), F32)
    for copy in stages:
        copy.wait()
    pl.semaphore_wait(barrier, CHIPS)

    def parts(a, head, source):
        if a == 0:
            return segown, segb.at[c, source]
        if a == 1:
            return kv_in.at[:, :, cols(head)], kvb.at[:, krows(c, source)]
        kind, low, high = GROUPS[a - 2]
        span = pl.ds(low, high - low)
        return qg_in.at[kind, span, :, cols(head)], qgb.at[kind, span, source]

    def in_copy(a, d):
        src, dst = parts(a, peer(d), z)
        return pltpu.make_async_remote_copy(
            src, dst, in_send.at[a, d], in_recv.at[a, d], device_id=chip(peer(d)), device_id_type=MESH)

    def in_arrival(a, d):
        src, dst = parts(a, z, lax.rem(z + CHIPS - d, CHIPS))
        return pltpu.make_async_remote_copy(
            src, dst, in_send.at[a, d], in_recv.at[a, d], device_id=chip(peer(d)), device_id_type=MESH)

    def own_copy(a):
        src, dst = parts(a, z, z)
        return pltpu.make_async_copy(src, dst, loc.at[a])

    turns = [a if a == b else jnp.where(c == 0, a, b) for a, b in ORDER]
    for a in range(2 + len(GROUPS)):
        for d in turns:
            in_copy(a, d).start()
        own_copy(a).start()

    def landed(a):
        own_copy(a).wait()
        for d in range(1, CHIPS):
            in_arrival(a, d).wait_recv()

    def forward(core, d):
        where = krows(core, lax.rem(z + CHIPS - d, CHIPS))
        return pltpu.make_async_remote_copy(
            kvb.at[:, where], kvb.at[:, where], fw_send.at[d], fw_recv.at[d], device_id=other, device_id_type=MESH)

    def seg_forward(core):
        return pltpu.make_async_remote_copy(
            segb.at[core], segb.at[core], fw_send.at[CHIPS], fw_recv.at[CHIPS], device_id=other, device_id_type=MESH)

    landed(0)
    seg_forward(c).start()
    lane = lax.broadcasted_iota(jnp.int32, (ROWS, HEAD_DIM), 1).astype(F32)

    def segment_rows(core, i):
        row = segb[core, i][0:1, :]
        return jnp.transpose(jnp.broadcast_to(row, (HEAD_DIM, 2 * HEAD_DIM)))[:ROWS]

    def own_rows(i, _):
        seg = segment_rows(c, i)
        eb[krows(c, i), :] = jnp.where(seg == lane, 1.0, 0.0).astype(BF16)
        hiding = jnp.where(lane > seg, HIDDEN, 0.0).astype(BF16)
        for j in range(BLOCKS):
            ab[j, i] = hiding[j * PIECE : (j + 1) * PIECE]
        return 0

    lax.fori_loop(0, CHIPS, own_rows, 0)
    seg_forward(c).wait_send()
    seg_forward(1 - c).wait_recv()

    def other_rows(i, _):
        eb[krows(1 - c, i), :] = jnp.where(segment_rows(1 - c, i) == lane, 1.0, 0.0).astype(BF16)
        return 0

    lax.fori_loop(0, CHIPS, other_rows, 0)
    vt[HEAD_DIM:, :] = jnp.ones((HEAD_DIM, ALL), BF16)

    own_copy(1).wait()
    forward(c, 0).start()
    for d in (1, 7, 2, 6, 3, 5, 4):
        in_arrival(1, d).wait_recv()
        forward(c, d).start()
    for d in range(CHIPS):
        forward(1 - c, d).wait_recv()
    for i in range(ALL // KC):
        at = slice(i * KC, (i + 1) * KC)
        vt[:HEAD_DIM, at] = jnp.transpose(kvb[1, at, :].astype(F32)).astype(BF16)
        kt[:, at] = jnp.transpose(kvb[0, at, :].astype(F32)).astype(BF16)

    def flat(ref, *i):
        return ref[i].reshape(RB, HEAD_DIM)

    def pieces(array):
        return array.reshape(CHIPS, PIECE, HEAD_DIM)

    def block(i):
        return pl.ds(pl.multiple_of(i * RB, RB), RB)

    def back(a, to, source):
        if a < 2:
            return kvg.at[a, rows(to)], kv_out.at[a, :, cols(source)]
        kind, low, high = GROUPS[a - 2]
        span = pl.ds(low, high - low)
        return oqb.at[kind, span, to], oq_out.at[kind, span, :, cols(source)]

    def out_copy(a, d):
        src, dst = back(a, peer(d), z)
        return pltpu.make_async_remote_copy(
            src, dst, out_send.at[a, d], out_recv.at[a, d], device_id=chip(peer(d)), device_id_type=MESH)

    def out_arrival(a, d):
        source = lax.rem(z + CHIPS - d, CHIPS)
        src, dst = back(a, source, source)
        return pltpu.make_async_remote_copy(
            src, dst, out_send.at[a, d], out_recv.at[a, d], device_id=chip(peer(d)), device_id_type=MESH)

    def out_own(a):
        src, dst = back(a, z, z)
        return pltpu.make_async_copy(src, dst, out_loc.at[a])

    def send_back(a):
        if a < 2:
            for to in range(CHIPS):

                @pl.when(to != z)
                def _():
                    out_copy(a, lax.rem(to - z + CHIPS, CHIPS)).start()

        else:
            for d in turns:
                out_copy(a, d).start()
        out_own(a).start()

    narrow = lax.broadcasted_iota(jnp.int32, (RB, HEAD_DIM), 1)
    ones = jnp.ones((KC, HEAD_DIM), BF16)

    def output_step(i, _):
        q = flat(qgb, 0, i)
        qx = jnp.concatenate([q, flat(ab, i)], axis=1)
        most = jnp.full((8, RB), -jnp.inf, F32)
        for j in range(ALL // KC):
            at = slice(j * KC, (j + 1) * KC)
            kx = jnp.concatenate([kvb[0, at, :], eb[at, :]], axis=1)
            s = dot_rows(kx, qx)
            sb[at, :] = s
            most = jnp.maximum(most, jnp.max(s.reshape(KC // 8, 8, RB), axis=0))
        top = jnp.max(most, axis=0, keepdims=True) * SCALE2
        for j in range(ALL // KC):
            at = slice(j * KC, (j + 1) * KC)
            pb[i, at, :] = jnp.exp2(sb[at, :] * SCALE2 - top).astype(BF16)
        both = jnp.transpose(dot_plain(vt[...], pb[i]))
        part = 1.0 / both[:, HEAD_DIM:]
        inv[block(i), :] = part
        oqb[0, i] = pieces((both[:, :HEAD_DIM] * part).astype(BF16))
        return 0

    def grad_step(i, _):
        low = flat(qgb, 1, i)
        part = inv[block(i), :]
        g = low.astype(F32)
        gn[block(i), :] = (g * part).astype(BF16)
        qn[block(i), :] = (flat(qgb, 0, i).astype(F32) * (part * SCALE)).astype(BF16)
        delta = -jnp.sum(g * flat(oqb, 0, i).astype(F32), axis=1, keepdims=True)
        first = delta.astype(BF16).astype(F32)
        second = (delta - first).astype(BF16).astype(F32)
        third = delta - first - second
        cells = jnp.where(narrow == 0, first, jnp.where(narrow == 1, second, jnp.where(narrow == 2, third, 0.0)))
        gx = jnp.concatenate([low, cells.astype(BF16)], axis=1)
        for j in range(ALL // KC):
            at = slice(j * KC, (j + 1) * KC)
            vx = jnp.concatenate([kvb[1, at, :], ones], axis=1)
            ds[i, at, :] = (pb[i, at, :].astype(F32) * dot_rows(vx, gx)).astype(BF16)
        dq = jnp.transpose(dot_plain(kt[...], ds[i]))
        oqb[1, i] = pieces((dq * (part * SCALE)).astype(BF16))
        return 0

    for group, (kind, low, high) in enumerate(GROUPS):
        landed(2 + group)
        lax.fori_loop(low, high, grad_step if kind else output_step, 0)
        send_back(2 + group)

    def terms(left, right, core, j):
        at = pl.ds(pl.multiple_of(core * OWN + j * RB, RB), RB)
        total = dot_plain(left[0, at, :], right[0:RB, :])
        for i in range(1, BLOCKS):
            total = total + dot_plain(left[i, at, :], right[i * RB : (i + 1) * RB, :])
        return total

    def swap(a, j):
        at = slice(j * RB, (j + 1) * RB)
        return pltpu.make_async_remote_copy(
            give.at[a, at], got.at[a, at], x_send.at[a, j], x_recv.at[a, j], device_id=other, device_id_type=MESH)

    sums = ((pb, gn), (ds, qn))
    for a, (left, right) in enumerate(sums):
        for j in range(BLOCKS):
            give[a, j * RB : (j + 1) * RB, :] = terms(left, right, 1 - c, j)
            swap(a, j).start()
    for a, (left, right) in enumerate(sums):
        for j in range(BLOCKS):
            mine = terms(left, right, c, j)
            swap(a, j).wait()
            at = slice(j * RB, (j + 1) * RB)
            kvg[a, at, :] = (mine + got[a, at, :]).astype(BF16)
        send_back(a)

    for a in range(2 + len(GROUPS)):
        for d in range(1, CHIPS):
            in_copy(a, d).wait_send()
    for d in range(CHIPS):
        forward(c, d).wait_send()
    for a in range(2 + len(GROUPS)):
        out_own(a).wait()
        for d in range(1, CHIPS):
            out_copy(a, d).wait_send()
            out_arrival(a, d).wait_recv()


def shards(queries, key_vectors, values, grad_output, segment_index):
    vmem, sems = pltpu.VMEM, pltpu.SemaphoreType.DMA
    any_spec = pl.BlockSpec(memory_space=pl.ANY)
    whole = jax.ShapeDtypeStruct(queries.shape, BF16)
    cut = (BLOCKS, PIECE, queries.shape[1])
    kinds = 2 + len(GROUPS)
    oq, kv = pl.pallas_call(
        kernel,
        out_shape=[vmem((2,) + cut, BF16), vmem((2,) + queries.shape, BF16)],
        in_specs=[any_spec] * 5,
        out_specs=[any_spec] * 2,
        scratch_shapes=[
            vmem((2,) + queries.shape, BF16),
            vmem((2,) + cut, BF16),
            vmem((2, ALL, HEAD_DIM), BF16),
            vmem((2, BLOCKS, CHIPS, PIECE, HEAD_DIM), BF16),
            vmem((1, ROWS), jnp.int32),
            vmem((8, 2 * HEAD_DIM), F32),
            vmem((2, CHIPS, 8, 2 * HEAD_DIM), F32),
            vmem((ALL, HEAD_DIM), BF16),
            vmem((BLOCKS, CHIPS, PIECE, HEAD_DIM), BF16),
            vmem((2 * HEAD_DIM, ALL), BF16),
            vmem((HEAD_DIM, ALL), BF16),
            vmem((ALL, RB), F32),
            vmem((BLOCKS, ALL, RB), BF16),
            vmem((BLOCKS, ALL, RB), BF16),
            vmem((OWN, HEAD_DIM), F32),
            vmem((OWN, HEAD_DIM), BF16),
            vmem((OWN, HEAD_DIM), BF16),
            vmem((2, OWN, HEAD_DIM), F32),
            vmem((2, OWN, HEAD_DIM), F32),
            vmem((2, BLOCKS, CHIPS, PIECE, HEAD_DIM), BF16),
            vmem((2, OWN, HEAD_DIM), BF16),
            sems,
            sems((4,)),
            sems((kinds, CHIPS)),
            sems((kinds, CHIPS)),
            sems((kinds,)),
            sems((CHIPS + 1,)),
            sems((CHIPS + 1,)),
            sems((kinds, CHIPS)),
            sems((kinds, CHIPS)),
            sems((kinds,)),
            sems((2, BLOCKS)),
            sems((2, BLOCKS)),
        ],
        compiler_params=pltpu.CompilerParams(
            collective_id=0, has_side_effects=True, vmem_limit_bytes=44 << 20
        ),
        cost_estimate=pl.CostEstimate(
            flops=12 * OWN * ALL * HEAD_DIM, bytes_accessed=8 * ROWS * 1024 * 2, transcendentals=OWN * ALL
        ),
    )(*[
        pltpu.with_memory_space_constraint(array, pltpu.HBM)
        for array in (
            queries.reshape(cut), key_vectors, values, grad_output.reshape(cut), segment_index.reshape(1, ROWS)
        )
    ])
    return pl.pallas_call(
        hand_over,
        out_shape=[whole] * 4,
        in_specs=[any_spec] * 2,
        out_specs=[any_spec] * 4,
        scratch_shapes=[sems((4,))],
    )(*[pltpu.with_memory_space_constraint(a.reshape((2,) + queries.shape), pltpu.VMEM) for a in (oq, kv)])


def hand_over(oq_ref, kv_ref, o_out, dq_out, dk_out, dv_out, sem):
    pairs = ((oq_ref.at[0], o_out), (oq_ref.at[1], dq_out), (kv_ref.at[0], dv_out), (kv_ref.at[1], dk_out))
    copies = [pltpu.make_async_copy(src, out, sem.at[a]) for a, (src, out) in enumerate(pairs)]
    for copy in copies:
        copy.start()
    for copy in copies:
        copy.wait()


def solution(mesh):
    wide = P(("dp", "frames"), "heads")
    return jax.shard_map(
        shards,
        mesh=mesh,
        in_specs=(wide, wide, wide, wide, P(("dp", "frames"))),
        out_specs=(wide, wide, wide, wide),
        check_vma=False,
    )
```

time: 72.4 us -> 70.3 us (0.971)
  Pallas kernels: 70.5 us -> 68.2 us
    pallas_call x2, Pallas kernels: 70.5 us -> 68.2 us  [the longest x1 67.1 us: shards(): pl.pallas_call(kernel, out_shape=[vmem((2,) + cut, BF16), vmem((2,) + que...]
where the time goes in v3:
time: 70.3 us; the launch traced here: 69 us
  Pallas kernels  68.2 us (97%)
  between operations  0.8 us (1%)
    pallas_call x1, Pallas kernels, shards(): pl.pallas_call(kernel, out_shape=[vmem((2,) + cut, BF16), vmem((2,) + que...  67.1 us

profile of v3, /device:TPU:2, one launch (start us, length us, event | category | flops | bytes accessed | tf_op | source)
XLA Modules:
  0.0 69.0 jit_solution(6800937454408103858)
XLA Ops:
  0.6 67.1 %shard_map.84 = (bf16[2,5,32,1024]{3,2,1,0:T(8,128)(2,1)S(1)}, bf16[2,160,1024]{2,1,0:T(8,128)(2,1)S(1)}) custom-call(bf16[5,32,1024]{2,1,0:T(8,128)(2,1)} %bitcast.5, bf16[160,1024]{1,0:T(8,128)(2,1)} %k_ref.1, bf16[160,1024]{1,0:T(8,128)(2,1)} %v_ref.1, bf16[5,32,1024]{2,1,0:T(8,128)(2,1)} %bitcast.6, s32[1,160]{1,0:T(1,128)} %bitcast.7), custom_call_target="tpu_custom_call" | custom-call | flops 5033164800 | bytes 2621440 | tf_op jit(solution)/shard_map/pallas_call | solution.py:303
  67.7 1.1 %shard_map.85 = (bf16[160,1024]{1,0:T(8,128)(2,1)}, bf16[160,1024]{1,0:T(8,128)(2,1)}, bf16[160,1024]{1,0:T(8,128)(2,1)}, bf16[160,1024]{1,0:T(8,128)(2,1)}) custom-call(bf16[2,160,1024]{2,1,0:T(8,128)(2,1)S(1)} %bitcast.4, bf16[2,160,1024]{2,1,0:T(8,128)(2,1)S(1)} %get-tuple-element.7.kv_ref), custom_call_target="tpu_custom_call" | custom-call | tf_op jit(solution)/shard_map/pallas_call | solution.py:355

commit v4 on v3

--- a/solution.py
+++ b/solution.py
@@ -95,12 +95,18 @@
     def in_copy(a, d):
         src, dst = parts(a, peer(d), z)
         return pltpu.make_async_remote_copy(
-            src, dst, in_send.at[a, d], in_recv.at[a, d], device_id=chip(peer(d)), device_id_type=MESH)
-
-    def in_arrival(a, d):
-        src, dst = parts(a, z, lax.rem(z + CHIPS - d, CHIPS))
-        return pltpu.make_async_remote_copy(
-            src, dst, in_send.at[a, d], in_recv.at[a, d], device_id=chip(peer(d)), device_id_type=MESH)
+            src, dst, in_send.at[a], in_recv.at[a], device_id=chip(peer(d)), device_id_type=MESH)
+
+    def in_all(a):
+        if a == 0:
+            size = segb.at[c, pl.ds(0, CHIPS - 1)]
+        elif a == 1:
+            size = kvb.at[:, pl.ds(0, (CHIPS - 1) * ROWS)]
+        else:
+            kind, low, high = GROUPS[a - 2]
+            size = qgb.at[kind, pl.ds(low, high - low), pl.ds(0, CHIPS - 1)]
+        return pltpu.make_async_remote_copy(
+            size, size, in_send.at[a], in_recv.at[a], device_id=other, device_id_type=MESH)
 
     def own_copy(a):
         src, dst = parts(a, z, z)
@@ -114,17 +120,16 @@
 
     def landed(a):
         own_copy(a).wait()
-        for d in range(1, CHIPS):
-            in_arrival(a, d).wait_recv()
-
-    def forward(core, d):
-        where = krows(core, lax.rem(z + CHIPS - d, CHIPS))
-        return pltpu.make_async_remote_copy(
-            kvb.at[:, where], kvb.at[:, where], fw_send.at[d], fw_recv.at[d], device_id=other, device_id_type=MESH)
+        in_all(a).wait_recv()
+
+    def forward(core):
+        where = pl.ds(pl.multiple_of(core * OWN, OWN), OWN)
+        return pltpu.make_async_remote_copy(
+            kvb.at[:, where], kvb.at[:, where], fw_send.at[0], fw_recv.at[0], device_id=other, device_id_type=MESH)
 
     def seg_forward(core):
         return pltpu.make_async_remote_copy(
-            segb.at[core], segb.at[core], fw_send.at[CHIPS], fw_recv.at[CHIPS], device_id=other, device_id_type=MESH)
+            segb.at[core], segb.at[core], fw_send.at[1], fw_recv.at[1], device_id=other, device_id_type=MESH)
 
     landed(0)
     seg_forward(c).start()
@@ -153,13 +158,9 @@
     lax.fori_loop(0, CHIPS, other_rows, 0)
     vt[HEAD_DIM:, :] = jnp.ones((HEAD_DIM, ALL), BF16)
 
-    own_copy(1).wait()
-    forward(c, 0).start()
-    for d in (1, 7, 2, 6, 3, 5, 4):
-        in_arrival(1, d).wait_recv()
-        forward(c, d).start()
-    for d in range(CHIPS):
-        forward(1 - c, d).wait_recv()
+    landed(1)
+    forward(c).start()
+    forward(1 - c).wait_recv()
     for i in range(ALL // KC):
         at = slice(i * KC, (i + 1) * KC)
         vt[:HEAD_DIM, at] = jnp.transpose(kvb[1, at, :].astype(F32)).astype(BF16)
@@ -184,13 +185,17 @@
     def out_copy(a, d):
         src, dst = back(a, peer(d), z)
         return pltpu.make_async_remote_copy(
-            src, dst, out_send.at[a, d], out_recv.at[a, d], device_id=chip(peer(d)), device_id_type=MESH)
-
-    def out_arrival(a, d):
-        source = lax.rem(z + CHIPS - d, CHIPS)
-        src, dst = back(a, source, source)
-        return pltpu.make_async_remote_copy(
-            src, dst, out_send.at[a, d], out_recv.at[a, d], device_id=chip(peer(d)), device_id_type=MESH)
+            src, dst, out_send.at[a], out_recv.at[a], device_id=chip(peer(d)), device_id_type=MESH)
+
+    def out_all(a):
+        seven = pl.ds(0, (CHIPS - 1) * HEAD_DIM)
+        if a < 2:
+            size = kv_out.at[a, :, seven]
+        else:
+            kind, low, high = GROUPS[a - 2]
+            size = oq_out.at[kind, pl.ds(low, high - low), :, seven]
+        return pltpu.make_async_remote_copy(
+            size, size, out_send.at[a], out_recv.at[a], device_id=other, device_id_type=MESH)
 
     def out_own(a):
         src, dst = back(a, z, z)
@@ -267,7 +272,7 @@
     def swap(a, j):
         at = slice(j * RB, (j + 1) * RB)
         return pltpu.make_async_remote_copy(
-            give.at[a, at], got.at[a, at], x_send.at[a, j], x_recv.at[a, j], device_id=other, device_id_type=MESH)
+            give.at[a, at], got.at[a, at], x_send.at[a], x_recv.at[a], device_id=other, device_id_type=MESH)
 
     sums = ((pb, gn), (ds, qn))
     for a, (left, right) in enumerate(sums):
@@ -276,22 +281,18 @@
             swap(a, j).start()
     for a, (left, right) in enumerate(sums):
         for j in range(BLOCKS):
-            mine = terms(left, right, c, j)
-            swap(a, j).wait()
-            at = slice(j * RB, (j + 1) * RB)
-            kvg[a, at, :] = (mine + got[a, at, :]).astype(BF16)
+            sb[j * RB : (j + 1) * RB, :HEAD_DIM] = terms(left, right, c, j)
+        pltpu.make_async_remote_copy(
+            give.at[a], got.at[a], x_send.at[a], x_recv.at[a], device_id=other, device_id_type=MESH).wait()
+        kvg[a] = (sb[:OWN, :HEAD_DIM] + got[a]).astype(BF16)
         send_back(a)
 
     for a in range(2 + len(GROUPS)):
-        for d in range(1, CHIPS):
-            in_copy(a, d).wait_send()
-    for d in range(CHIPS):
-        forward(c, d).wait_send()
+        in_all(a).wait_send()
+    forward(c).wait_send()
     for a in range(2 + len(GROUPS)):
         out_own(a).wait()
-        for d in range(1, CHIPS):
-            out_copy(a, d).wait_send()
-            out_arrival(a, d).wait_recv()
+        out_all(a).wait()
 
 
 def shards(queries, key_vectors, values, grad_output, segment_index):
@@ -329,16 +330,16 @@
             vmem((2, OWN, HEAD_DIM), BF16),
             sems,
             sems((4,)),
-            sems((kinds, CHIPS)),
-            sems((kinds, CHIPS)),
-            sems((kinds,)),
-            sems((CHIPS + 1,)),
-            sems((CHIPS + 1,)),
-            sems((kinds, CHIPS)),
-            sems((kinds, CHIPS)),
-            sems((kinds,)),
-            sems((2, BLOCKS)),
-            sems((2, BLOCKS)),
+            sems((kinds,)),
+            sems((kinds,)),
+            sems((kinds,)),
+            sems((2,)),
+            sems((2,)),
+            sems((kinds,)),
+            sems((kinds,)),
+            sems((kinds,)),
+            sems((2,)),
+            sems((2,)),
         ],
         compiler_params=pltpu.CompilerParams(
             collective_id=0, has_side_effects=True, vmem_limit_bytes=44 << 20

time: 70.3 us -> 68.2 us (0.970)
  Pallas kernels: 68.2 us -> 66.3 us
    pallas_call x1, Pallas kernels: 67.1 us -> 65.3 us  [shards(): pl.pallas_call(kernel, out_shape=[vmem((2,) + cut, BF16), vmem((2,) + que...]
where the time goes in v4:
time: 68.2 us; the launch traced here: 67 us
  Pallas kernels  66.3 us (97%)
    pallas_call x1, Pallas kernels, shards(): pl.pallas_call(kernel, out_shape=[vmem((2,) + cut, BF16), vmem((2,) + que...  65.3 us

profile of v4, /device:TPU:2, one launch (start us, length us, event | category | flops | bytes accessed | tf_op | source)
XLA Modules:
  0.0 67.0 jit_solution(12731022106359324183)
XLA Ops:
  0.6 65.3 %shard_map.84 = (bf16[2,5,32,1024]{3,2,1,0:T(8,128)(2,1)S(1)}, bf16[2,160,1024]{2,1,0:T(8,128)(2,1)S(1)}) custom-call(bf16[5,32,1024]{2,1,0:T(8,128)(2,1)} %bitcast.5, bf16[160,1024]{1,0:T(8,128)(2,1)} %k_ref.1, bf16[160,1024]{1,0:T(8,128)(2,1)} %v_ref.1, bf16[5,32,1024]{2,1,0:T(8,128)(2,1)} %bitcast.6, s32[1,160]{1,0:T(1,128)} %bitcast.7), custom_call_target="tpu_custom_call" | custom-call | flops 5033164800 | bytes 2621440 | tf_op jit(solution)/shard_map/pallas_call | solution.py:304
  65.9 1.1 %shard_map.85 = (bf16[160,1024]{1,0:T(8,128)(2,1)}, bf16[160,1024]{1,0:T(8,128)(2,1)}, bf16[160,1024]{1,0:T(8,128)(2,1)}, bf16[160,1024]{1,0:T(8,128)(2,1)}) custom-call(bf16[2,160,1024]{2,1,0:T(8,128)(2,1)S(1)} %bitcast.4, bf16[2,160,1024]{2,1,0:T(8,128)(2,1)S(1)} %get-tuple-element.7.kv_ref), custom_call_target="tpu_custom_call" | custom-call | tf_op jit(solution)/shard_map/pallas_call | solution.py:356

commit v5 on v4

--- a/solution.py
+++ b/solution.py
@@ -1,4 +1,3 @@
-import functools
 import math
 
 import jax
@@ -21,7 +20,7 @@
 SCALE2 = SCALE * math.log2(math.e)
 PIECE = RB // CHIPS
 BLOCKS = OWN // RB
-GROUPS = ((0, 0, 2), (0, 2, 5), (1, 0, 3), (1, 3, 5))
+GROUPS = ((0, 0, 3), (0, 3, 5), (1, 0, 2), (1, 2, 4), (1, 4, 5))
 ORDER = ((4, 4), (3, 5), (5, 3), (2, 6), (6, 2), (1, 7), (7, 1))
 FAR_FIRST = (4, 3, 5, 2, 6, 1, 7)
 F32, BF16 = jnp.float32, jnp.bfloat16
@@ -61,6 +60,10 @@
     def krows(core, i):
         return pl.ds(pl.multiple_of((core * CHIPS + i) * ROWS, ROWS), ROWS)
 
+    barrier = pltpu.get_barrier_semaphore()
+    for d in FAR_FIRST:
+        pl.semaphore_signal(barrier, inc=1, device_id=chip(peer(d)), device_id_type=MESH)
+    pl.semaphore_signal(barrier, inc=1, device_id=other, device_id_type=MESH)
     seg_copy = pltpu.make_async_copy(seg_ref, segin, seg_sem)
     seg_copy.start()
     stages = [
@@ -71,16 +74,9 @@
     ]
     for copy in stages:
         copy.start()
-
-    barrier = pltpu.get_barrier_semaphore()
-    for d in FAR_FIRST:
-        pl.semaphore_signal(barrier, inc=1, device_id=chip(peer(d)), device_id_type=MESH)
-    pl.semaphore_signal(barrier, inc=1, device_id=other, device_id_type=MESH)
     seg_copy.wait()
     segown[:, :ROWS] = jnp.broadcast_to(segin[...].astype(F32), (8, ROWS))
     segown[:, ROWS:] = jnp.zeros((8, 2 * HEAD_DIM - ROWS), F32)
-    for copy in stages:
-        copy.wait()
     pl.semaphore_wait(barrier, CHIPS)
 
     def parts(a, head, source):
@@ -114,6 +110,9 @@
 
     turns = [a if a == b else jnp.where(c == 0, a, b) for a, b in ORDER]
     for a in range(2 + len(GROUPS)):
+        if a in (1, 2):
+            for copy in stages[2 * a - 2 : 2 * a]:
+                copy.wait()
         for d in turns:
             in_copy(a, d).start()
         own_copy(a).start()

time: 68.2 us -> 68.2 us (level)
  the two profiles are of different devices: /device:TPU:2 before, /device:TPU:65 now
where the time goes in v5:
time: 68.2 us; the launch traced here: 68.1 us
  Pallas kernels  67.5 us (99%)
    pallas_call x1, Pallas kernels, shards(): pl.pallas_call(kernel, out_shape=[vmem((2,) + cut, BF16), vmem((2,) + que...  66.4 us

profile of v5, /device:TPU:65, one launch (start us, length us, event | category | flops | bytes accessed | tf_op | source)
XLA Modules:
  0.0 68.1 jit_solution(15529151045473791390)
XLA Ops:
  0.6 66.4 %shard_map.84 = (bf16[2,5,32,1024]{3,2,1,0:T(8,128)(2,1)S(1)}, bf16[2,160,1024]{2,1,0:T(8,128)(2,1)S(1)}) custom-call(bf16[5,32,1024]{2,1,0:T(8,128)(2,1)} %bitcast.5, bf16[160,1024]{1,0:T(8,128)(2,1)} %k_ref.1, bf16[160,1024]{1,0:T(8,128)(2,1)} %v_ref.1, bf16[5,32,1024]{2,1,0:T(8,128)(2,1)} %bitcast.6, s32[1,160]{1,0:T(1,128)} %bitcast.7), custom_call_target="tpu_custom_call" | custom-call | flops 5033164800 | bytes 2621440 | tf_op jit(solution)/shard_map/pallas_call | solution.py:303
  67.0 1.1 %shard_map.85 = (bf16[160,1024]{1,0:T(8,128)(2,1)}, bf16[160,1024]{1,0:T(8,128)(2,1)}, bf16[160,1024]{1,0:T(8,128)(2,1)}, bf16[160,1024]{1,0:T(8,128)(2,1)}) custom-call(bf16[2,160,1024]{2,1,0:T(8,128)(2,1)S(1)} %bitcast.4, bf16[2,160,1024]{2,1,0:T(8,128)(2,1)S(1)} %get-tuple-element.7.kv_ref), custom_call_target="tpu_custom_call" | custom-call | tf_op jit(solution)/shard_map/pallas_call | solution.py:355

commit v6 on v4

--- a/solution.py
+++ b/solution.py
@@ -40,7 +40,7 @@
     oq_out, kv_out,
     kv_in, qg_in, kvb, qgb, segin, segown, segb, eb, ab, vt, kt, sb, pb, ds, inv, gn, qn,
     give, got, oqb, kvg,
-    seg_sem, stage, in_send, in_recv, loc, fw_send, fw_recv, out_send, out_recv, out_loc, x_send, x_recv,
+    seg_sem, stage, in_send, in_recv, fw_send, fw_recv, out_send, out_recv, x_send, x_recv,
 ):
     me = lax.axis_index("frames")
     z, c = me // 2, lax.rem(me, 2)
@@ -95,22 +95,22 @@
     def in_copy(a, d):
         src, dst = parts(a, peer(d), z)
         return pltpu.make_async_remote_copy(
-            src, dst, in_send.at[a], in_recv.at[a], device_id=chip(peer(d)), device_id_type=MESH)
+            src, dst, in_send, in_recv.at[a], device_id=chip(peer(d)), device_id_type=MESH)
 
     def in_all(a):
         if a == 0:
-            size = segb.at[c, pl.ds(0, CHIPS - 1)]
+            size = segb.at[c]
         elif a == 1:
-            size = kvb.at[:, pl.ds(0, (CHIPS - 1) * ROWS)]
+            size = kvb.at[:, pl.ds(0, OWN)]
         else:
             kind, low, high = GROUPS[a - 2]
-            size = qgb.at[kind, pl.ds(low, high - low), pl.ds(0, CHIPS - 1)]
-        return pltpu.make_async_remote_copy(
-            size, size, in_send.at[a], in_recv.at[a], device_id=other, device_id_type=MESH)
+            size = qgb.at[kind, pl.ds(low, high - low)]
+        return pltpu.make_async_remote_copy(
+            size, size, in_send, in_recv.at[a], device_id=other, device_id_type=MESH)
 
     def own_copy(a):
         src, dst = parts(a, z, z)
-        return pltpu.make_async_copy(src, dst, loc.at[a])
+        return pltpu.make_async_copy(src, dst, in_recv.at[a])
 
     turns = [a if a == b else jnp.where(c == 0, a, b) for a, b in ORDER]
     for a in range(2 + len(GROUPS)):
@@ -119,7 +119,6 @@
         own_copy(a).start()
 
     def landed(a):
-        own_copy(a).wait()
         in_all(a).wait_recv()
 
     def forward(core):
@@ -185,21 +184,20 @@
     def out_copy(a, d):
         src, dst = back(a, peer(d), z)
         return pltpu.make_async_remote_copy(
-            src, dst, out_send.at[a], out_recv.at[a], device_id=chip(peer(d)), device_id_type=MESH)
+            src, dst, out_send, out_recv.at[a], device_id=chip(peer(d)), device_id_type=MESH)
 
     def out_all(a):
-        seven = pl.ds(0, (CHIPS - 1) * HEAD_DIM)
         if a < 2:
-            size = kv_out.at[a, :, seven]
+            size = kv_out.at[a]
         else:
             kind, low, high = GROUPS[a - 2]
-            size = oq_out.at[kind, pl.ds(low, high - low), :, seven]
-        return pltpu.make_async_remote_copy(
-            size, size, out_send.at[a], out_recv.at[a], device_id=other, device_id_type=MESH)
+            size = oq_out.at[kind, pl.ds(low, high - low)]
+        return pltpu.make_async_remote_copy(
+            size, size, out_send, out_recv.at[a], device_id=other, device_id_type=MESH)
 
     def out_own(a):
         src, dst = back(a, z, z)
-        return pltpu.make_async_copy(src, dst, out_loc.at[a])
+        return pltpu.make_async_copy(src, dst, out_recv.at[a])
 
     def send_back(a):
         if a < 2:
@@ -288,11 +286,12 @@
         send_back(a)
 
     for a in range(2 + len(GROUPS)):
-        in_all(a).wait_send()
+        out_all(a).wait_recv()
     forward(c).wait_send()
-    for a in range(2 + len(GROUPS)):
-        out_own(a).wait()
-        out_all(a).wait()
+    for sem, sent in ((in_send, 7 * 172032), (out_send, 7 * 163840)):
+        size = pb.at[0, pl.ds(0, sent // 512)]
+        pltpu.make_async_remote_copy(
+            size, size, sem, in_recv.at[0], device_id=other, device_id_type=MESH).wait_send()
 
 
 def shards(queries, key_vectors, values, grad_output, segment_index):
@@ -330,13 +329,11 @@
             vmem((2, OWN, HEAD_DIM), BF16),
             sems,
             sems((4,)),
-            sems((kinds,)),
-            sems((kinds,)),
+            sems,
             sems((kinds,)),
             sems((2,)),
             sems((2,)),
-            sems((kinds,)),
-            sems((kinds,)),
+            sems,
             sems((kinds,)),
             sems((2,)),
             sems((2,)),

time: 68.2 us -> 68 us (level)
  no operation moved by 1% of the time
where the time goes in v6:
time: 68 us; the launch traced here: 66.8 us
  Pallas kernels  66.2 us (97%)
    pallas_call x1, Pallas kernels, shards(): pl.pallas_call(kernel, out_shape=[vmem((2,) + cut, BF16), vmem((2,) + que...  65.1 us

profile of v6, /device:TPU:2, one launch (start us, length us, event | category | flops | bytes accessed | tf_op | source)
XLA Modules:
  0.0 66.8 jit_solution(3628948483136961950)
XLA Ops:
  0.6 65.1 %shard_map.84 = (bf16[2,5,32,1024]{3,2,1,0:T(8,128)(2,1)S(1)}, bf16[2,160,1024]{2,1,0:T(8,128)(2,1)S(1)}) custom-call(bf16[5,32,1024]{2,1,0:T(8,128)(2,1)} %bitcast.5, bf16[160,1024]{1,0:T(8,128)(2,1)} %k_ref.1, bf16[160,1024]{1,0:T(8,128)(2,1)} %v_ref.1, bf16[5,32,1024]{2,1,0:T(8,128)(2,1)} %bitcast.6, s32[1,160]{1,0:T(1,128)} %bitcast.7), custom_call_target="tpu_custom_call" | custom-call | flops 5033164800 | bytes 2621440 | tf_op jit(solution)/shard_map/pallas_call | solution.py:303
  65.7 1.1 %shard_map.85 = (bf16[160,1024]{1,0:T(8,128)(2,1)}, bf16[160,1024]{1,0:T(8,128)(2,1)}, bf16[160,1024]{1,0:T(8,128)(2,1)}, bf16[160,1024]{1,0:T(8,128)(2,1)}) custom-call(bf16[2,160,1024]{2,1,0:T(8,128)(2,1)S(1)} %bitcast.4, bf16[2,160,1024]{2,1,0:T(8,128)(2,1)S(1)} %get-tuple-element.7.kv_ref), custom_call_target="tpu_custom_call" | custom-call | tf_op jit(solution)/shard_map/pallas_call | solution.py:353
